TPU v7x, 512 devices: a whole 4x8x8 slice. The times are simulated.
512 devices in a mesh: seq: 128 (over z, x, y_lo, core), loc: 4 (over y_hi).
Axes of the slice: x: 4, y: 8 (y_hi: 4, y_lo: 2; y = y_hi * 2 + y_lo), z: 8, core: 2. Of those that a mesh axis runs over, the one named last changes fastest.
Arguments:
- queries: bfloat16 [3840, 4096], P('seq', 'loc'), may hold values from -32 to 32
- keys: bfloat16 [3840, 4096], P('seq', 'loc'), may hold values from -32 to 32
- values: bfloat16 [3840, 4096], P('seq', 'loc'), may hold values from -6 to 6
- positions: int32 [3840], P('seq'), may hold values from 0 to 3839, as said below
- byte_embed: bfloat16 [30720, 1024], P('seq', 'loc'), may hold values from -6 to 6
- w_slot: bfloat16 [512, 1024], replicated, may hold values from -0.25 to 0.25
- gain: float32 [1024], P('loc'), may hold values from 0.1 to 1.9
Outputs:
- local_input: bfloat16 [30720, 1024], P('seq', 'loc')
Inputs may be any that keep to these rules, and one draw needn't show every extreme that they name: positions is a permutation of the patch positions; each aligned run of 15 rows holds consecutive ascending positions.
All inputs are finite; a program needn't handle non-finite values.
Results may differ from a plain program's by a relative error of at most 0.0065.
Values may be sent and summed in bfloat16 or wider, within the bound.
No kernel may reach another device: no remote copies, remote signals or barrier semaphores. Data moves between devices by JAX's collectives and lax.ppermute only.
A program may use at most 128 MiB of HBM per device.

v0:
```python
import math

import jax
import jax.numpy as jnp
from jax import lax
from jax.sharding import PartitionSpec as P

HEAD_DIM = 128
PATCH = 8
LOCAL_D = 1024
SLOT_D = 512


def passed_along(shard, axis, by):
    length = lax.axis_size(axis)
    return lax.ppermute(shard, axis, [(i, (i + by) % length) for i in range(length)])


def update_state(carry_state, query_heads, query_pos, key_block, value_block, key_pos):
    running_max, running_sum, running_acc = carry_state
    key_count = key_block.shape[0]
    heads_here = query_heads.shape[1]
    key_heads = key_block.reshape(key_count, heads_here, HEAD_DIM)
    value_heads = value_block.reshape(key_count, heads_here, HEAD_DIM).astype(jnp.float32)
    scores = jnp.einsum("qhd,khd->hqk", query_heads, key_heads, preferred_element_type=jnp.float32)
    scores = scores * (1.0 / math.sqrt(HEAD_DIM))
    allowed = (key_pos[None, :] <= query_pos[:, None])[None, :, :]
    masked = jnp.where(allowed, scores, jnp.float32(-1e30))
    new_max = jnp.maximum(running_max, jnp.max(masked, axis=-1))
    weights = jnp.where(allowed, jnp.exp(scores - new_max[:, :, None]), jnp.float32(0.0))
    rescale = jnp.exp(running_max - new_max)
    new_sum = running_sum * rescale + jnp.sum(weights, axis=-1)
    new_acc = running_acc * rescale[:, :, None] + jnp.einsum("hqk,khd->hqd", weights, value_heads)
    return (new_max, new_sum, new_acc)


def absorb(carry_state, query_heads, query_pos, key_block, value_block, key_pos):
    return update_state(carry_state, query_heads, query_pos, key_block, value_block, key_pos)


def on_device(queries, keys, values, positions, byte_embed, w_slot, gain):
    row_count = queries.shape[0]
    heads_here = queries.shape[1] // HEAD_DIM
    query_heads = queries.reshape(row_count, heads_here, HEAD_DIM)
    every_pos = lax.all_gather(positions, "seq", axis=0, tiled=True)
    cycle_size = lax.axis_size("seq")
    my_index = lax.axis_index("seq")
    initial = (
        jnp.full((heads_here, row_count), -1e30, jnp.float32),
        jnp.zeros((heads_here, row_count), jnp.float32),
        jnp.zeros((heads_here, row_count, HEAD_DIM), jnp.float32),
    )
    first = absorb(initial, query_heads, positions, keys, values, positions)

    def cycle_turn(turn_index, carried):
        carry_state, held_keys, held_values = carried
        held_keys, held_values = passed_along((held_keys, held_values), "seq", 1)
        source = (my_index - turn_index) % cycle_size
        key_pos = lax.dynamic_slice_in_dim(every_pos, source * row_count, row_count)
        carry_state = absorb(carry_state, query_heads, positions, held_keys, held_values, key_pos)
        return (carry_state, held_keys, held_values)

    final_state, unused_keys, unused_values = lax.fori_loop(
        1, cycle_size, cycle_turn, (first, keys, values)
    )
    running_max, running_sum, running_acc = final_state
    summed = running_acc / running_sum[:, :, None]
    attended = (
        jnp.transpose(summed, (1, 0, 2))
        .reshape(row_count, heads_here * HEAD_DIM)
        .astype(jnp.bfloat16)
    )
    slot_count = attended.shape[1] // SLOT_D
    my_slots = attended.reshape(row_count * slot_count, SLOT_D)
    projected = jnp.dot(my_slots, w_slot, preferred_element_type=jnp.float32)
    projected = projected.reshape(row_count, slot_count, w_slot.shape[1])
    columns = lax.all_to_all(projected, "loc", split_axis=2, concat_axis=1, tiled=True)
    mixed = columns.reshape(row_count * PATCH, columns.shape[2]) + byte_embed.astype(jnp.float32)
    row_squares = lax.psum(jnp.sum(mixed * mixed, axis=-1, keepdims=True), "loc")
    spread = row_squares / LOCAL_D + 1e-05
    return (mixed / jnp.sqrt(spread) * gain[None, :]).astype(jnp.bfloat16)


def solution(mesh):
    placed = (
        P("seq", "loc"),
        P("seq", "loc"),
        P("seq", "loc"),
        P("seq"),
        P("seq", "loc"),
        P(),
        P("loc"),
    )
    return jax.shard_map(
        on_device, mesh=mesh, in_specs=placed, out_specs=P("seq", "loc"), check_vma=False
    )
```

profile of v0, /device:TPU:16, one launch (start us, length us, event | category | flops | bytes accessed | tf_op | source)
XLA Modules:
  0.0 2164.0 jit_solution(17534955945619735356)
XLA Ops:
  5.2 560.0 %all-reduce = s32[3840]{0:T(1024)S(1)} all-reduce(s32[3840]{0:T(1024)S(1)} %dynamic-update-slice), channel_id=1, replica_groups=mesh['seq'=128,'loc'=4] {'seq'}, use_global_device_ids=true, to_apply=%add | all-reduce | flops 3840 | bytes 30720
  565.5 1564.2 %while.23 = (s32[]{:T(128)}, f32[8,30]{1,0:T(8,128)S(1)}, f32[8,30]{1,0:T(8,128)S(1)}, f32[8,30,128]{2,1,0:T(8,128)S(1)}, bf16[30,1024]{1,0:T(8,128)(2,1)S(1)}, ...) while((s32[]{:T(128)}, f32[8,30]{1,0:T(8,128)S(1)}, ...), condition=%wide.region_5.6_spmd, body=%wide.region_2.5_spmd.sunk | while | flops 3806838 | bytes 1781504 | solution.py:63
  581.8 5.8 collective-permute-done
  594.2 5.8 collective-permute-done
  606.5 5.8 collective-permute-done
  655.7 5.8 collective-permute-done
  668.1 5.8 collective-permute-done
  680.4 5.8 collective-permute-done
  692.7 5.8 collective-permute-done
  729.6 5.8 collective-permute-done
  742.0 5.8 collective-permute-done
  766.6 5.8 collective-permute-done
  803.5 5.8 collective-permute-done
  815.9 5.8 collective-permute-done
  828.2 5.8 collective-permute-done
  889.8 5.8 collective-permute-done
  902.1 5.8 collective-permute-done
  963.7 5.8 collective-permute-done
  976.0 5.8 collective-permute-done
  1037.5 5.8 collective-permute-done
  1049.9 5.8 collective-permute-done
  1099.1 5.8 collective-permute-done
  1111.4 5.8 collective-permute-done
  1123.8 5.8 collective-permute-done
  1136.1 5.8 collective-permute-done
  1173.0 5.8 collective-permute-done
  1185.3 5.8 collective-permute-done
  1197.7 5.8 collective-permute-done
  1210.0 5.8 collective-permute-done
  1246.9 5.8 collective-permute-done
  1259.2 5.8 collective-permute-done
  1271.6 5.8 collective-permute-done
  1283.9 5.8 collective-permute-done
  1333.1 5.8 collective-permute-done
  1345.5 5.8 collective-permute-done
  1407.0 5.8 collective-permute-done
  1419.4 5.8 collective-permute-done
  1480.9 5.8 collective-permute-done
  1493.3 5.8 collective-permute-done
  1554.8 5.8 collective-permute-done
  1567.2 5.8 collective-permute-done
  1579.5 5.8 collective-permute-done
  1616.4 5.8 collective-permute-done
  1641.1 5.8 collective-permute-done
  1653.4 5.8 collective-permute-done
  1690.3 5.8 collective-permute-done
  2132.6 13.0 all_to_all.15
  2150.9 11.7 psum.7
  (2287 shorter events, 1307.5 us)
Async XLA Ops:
  602.4 9.8 collective-permute-start
  616.7 9.8 collective-permute-start.1
  664.0 9.8 collective-permute-start
  665.9 9.8 collective-permute-start.1
  688.7 9.8 collective-permute-start
  690.6 9.8 collective-permute-start.1
  737.9 9.8 collective-permute-start
  752.2 9.8 collective-permute-start.1
  762.6 9.8 collective-permute-start
  764.5 9.8 collective-permute-start.1
  824.1 9.8 collective-permute-start
  826.1 9.8 collective-permute-start.1
  898.0 9.8 collective-permute-start
  900.0 9.8 collective-permute-start.1
  971.9 9.8 collective-permute-start
  973.9 9.8 collective-permute-start.1
  1045.8 9.8 collective-permute-start
  1060.1 9.8 collective-permute-start.1
  1132.0 9.8 collective-permute-start
  1134.0 9.8 collective-permute-start.1
  1181.3 9.8 collective-permute-start
  1205.9 9.8 collective-permute-start
  1207.9 9.8 collective-permute-start.1
  1267.5 9.8 collective-permute-start
  1269.5 9.8 collective-permute-start.1
  1279.8 9.8 collective-permute-start
  1281.8 9.8 collective-permute-start.1
  1341.4 9.8 collective-permute-start
  1343.3 9.8 collective-permute-start.1
  1368.0 9.8 collective-permute-start.1
  1415.3 9.8 collective-permute-start
  1417.2 9.8 collective-permute-start.1
  1489.2 9.8 collective-permute-start
  1503.5 9.8 collective-permute-start.1
  1575.4 9.8 collective-permute-start
  1577.4 9.8 collective-permute-start.1
  1649.3 9.8 collective-permute-start
  1651.3 9.8 collective-permute-start.1
  1723.2 9.8 collective-permute-start
  1725.2 9.8 collective-permute-start.1
  1784.8 9.8 collective-permute-start
  1786.7 9.8 collective-permute-start.1
  1797.1 9.8 collective-permute-start
  1811.4 9.8 collective-permute-start.1
  1858.7 9.8 collective-permute-start
  1860.6 9.8 collective-permute-start.1
  1883.3 9.8 collective-permute-start
  1885.3 9.8 collective-permute-start.1
  (212 other events, 4153.5 us)
where the time goes:
time: 2170 us; the launch traced here: 2160 us
  waiting for transfers between devices  973 us (45%)
  blocking collectives  585 us (27%)
  starting transfers between devices  488 us (22%)
  matrix products  52.7 us (2%)
  local copies, waits for them, and re-layouts  27.7 us (1%)
    ppermute x254, waiting for transfers between devices, passed_along(): lax.ppermute(shard, axis, [(i, (i + by) % length) for i in range(length)])  973 us
    unnamed x1, blocking collectives  560 us
    ppermute x254, starting transfers between devices, passed_along(): lax.ppermute(shard, axis, [(i, (i + by) % length) for i in range(length)])  488 us
  transfers between devices with their start and end apart: 254, of which 254 were waited for; matrix products, arithmetic and copies ran while one was open for 1% of the time, Pallas kernels for 0%

commit v1 on v0

v1 whole, which is shorter than its diff:
```python
import math

import jax
import jax.numpy as jnp
from jax import lax
from jax.experimental import pallas as pl
from jax.experimental.pallas import tpu as pltpu
from jax.sharding import Mesh
from jax.sharding import PartitionSpec as P

HEAD_DIM = 128
PATCH = 8
RUN = 15
RUNS = 2
ROWS = RUN * RUNS
TILE = 16
PAD = RUNS * TILE
CHUNK = 8
CHUNKS = 4
HEADS_HERE = 8
LOCAL_D = 1024
SLOT_D = 512
LOCS = 4
COLS = LOCAL_D // LOCS
SEQ = ("za", "zb", "zc", "x", "yl", "c")
GROUP = ("za", "zb", "zc", "x", "yl")
PEERS = RUNS * CHUNKS * HEADS_HERE
QN = PEERS * TILE
KN = PEERS * CHUNK
STEP = 256
FLOOR = -1e20
MASKED = -1e30
FAR = 1e6
bf16 = jnp.bfloat16
f32 = jnp.float32


def iota(shape, dim):
    return lax.broadcasted_iota(jnp.int32, shape, dim)


def pick(condition, rows):
    select = jnp.where(condition, f32(1), f32(0)).astype(bf16)
    return jnp.dot(select, rows, preferred_element_type=f32)


def three_parts(x):
    high = x.astype(bf16).astype(f32)
    middle = (x - high).astype(bf16).astype(f32)
    return high, middle, x - high - middle


def pack(
    pos_hbm, q_hbm, k_hbm, v_hbm, e_hbm, gain_hbm, out_ref, e_out, pos_ref, q_ref, k_ref, v_ref, e_ref, gain_ref, sems
):
    pairs = [
        (pos_hbm, pos_ref),
        (q_hbm, q_ref),
        (k_hbm, k_ref),
        (v_hbm, v_ref),
        (e_hbm, e_ref),
        (gain_hbm, gain_ref),
    ]
    copies = [pltpu.make_async_copy(a, b, sems.at[n]) for n, (a, b) in enumerate(pairs)]
    for copy in copies:
        copy.start()
    for copy in copies[:2]:
        copy.wait()

    wide = (PAD, HEADS_HERE * HEAD_DIM)
    to, source = iota((PAD, ROWS), 0), iota((PAD, ROWS), 1)
    place = to % TILE
    queries = pick((source == to // TILE * RUN + place) & (place < RUN), q_ref[...])
    first = (pos_ref[0] // RUN).astype(f32)
    second = (pos_ref[RUN] // RUN).astype(f32)
    numbers = jnp.where(iota(wide, 1) % HEAD_DIM < HEAD_DIM // 2, first, second)
    queries = jnp.where(iota(wide, 0) % TILE == RUN, numbers, queries).astype(bf16)

    for copy in copies[2:4]:
        copy.wait()
    to, source = iota((CHUNKS * TILE, ROWS), 0), iota((CHUNKS * TILE, ROWS), 1)
    place = to % TILE
    row = to // TILE * CHUNK + place % CHUNK
    both = pick((source == row) & (place < CHUNK), k_ref[...])
    both = (both + pick((source == row) & (place >= CHUNK), v_ref[...])).astype(bf16)
    for z in range(RUNS * CHUNKS):
        i, j = z // CHUNKS, z % CHUNKS
        for h in range(HEADS_HERE):
            cols = slice(h * HEAD_DIM, (h + 1) * HEAD_DIM)
            out_ref[z * HEADS_HERE + h, 0:TILE, :] = queries[i * TILE : (i + 1) * TILE, cols]
            out_ref[z * HEADS_HERE + h, TILE : 2 * TILE, :] = both[j * TILE : (j + 1) * TILE, cols]

    for copy in copies[4:]:
        copy.wait()
    height, rows = LOCS * 2 * PAD, ROWS * PATCH
    to, source = iota((height, rows), 0), iota((height, rows), 1)
    place = to % TILE
    patch = to // TILE % RUNS * RUN + place
    moved = pick((source == patch * PATCH + to // PAD) & (place < RUN), e_ref[...])
    high, middle, low = three_parts(gain_ref[...])
    row = iota((height, COLS), 0) % (2 * PAD)
    moved = jnp.where(row == RUN, high, moved)
    moved = jnp.where(row == TILE + RUN, middle, moved)
    moved = jnp.where(row == PAD + RUN, low, moved)
    e_out[...] = moved.astype(bf16).reshape(LOCS, 2 * PAD, COLS)


def split(in_ref, out_ref):
    both = in_ref[:, TILE : 2 * TILE, :].astype(f32)
    out_ref[0:KN, :] = both[:, 0:CHUNK, :].reshape(KN, HEAD_DIM).astype(bf16)
    out_ref[KN : 2 * KN, :] = both[:, CHUNK:TILE, :].reshape(KN, HEAD_DIM).astype(bf16)
    numbers = in_ref[:, 0:TILE, :].astype(f32)[:, RUN:TILE, :]
    out_ref[2 * KN : 2 * KN + PEERS, :] = numbers.reshape(PEERS, HEAD_DIM).astype(bf16)


def run_starts(numbers):
    other = pltpu.roll(numbers, HEAD_DIM // 2, 1)
    lower = iota(numbers.shape, 1) < HEAD_DIM // 2
    return jnp.where(lower, numbers, other) * RUN, jnp.where(lower, other, numbers) * RUN


def key_positions(numbers, chunk):
    first, second = run_starts(numbers)
    dims = (PEERS, CHUNK, HEAD_DIM)
    row = iota(dims, 1) + chunk * CHUNK
    place = row.astype(f32)
    pos = jnp.where(
        row < RUN,
        jnp.broadcast_to(first[:, None, :], dims) + place,
        jnp.broadcast_to(second[:, None, :], dims) + (place - RUN),
    )
    return jnp.where(row < ROWS, pos, f32(FAR)).reshape(KN, HEAD_DIM)


def query_positions(numbers, run):
    first, second = run_starts(numbers)
    start = jnp.where(run == 0, first, second)
    dims = (PEERS, TILE, HEAD_DIM)
    row = iota(dims, 1)
    pos = jnp.broadcast_to(start[:, None, :], dims) + row.astype(f32)
    return jnp.where(row < RUN, pos, f32(-1)).reshape(QN, HEAD_DIM)


def attend(in_ref, kv_ref, out_ref, s_ref):
    scale = math.log2(math.e) / math.sqrt(HEAD_DIM)
    run = lax.axis_index("za")
    chunk = lax.axis_index("zb") * 2 + lax.axis_index("zc")
    queries = in_ref[:, 0:TILE, :]
    numbers = queries.astype(f32)[:, RUN:TILE, :].reshape(PEERS, HEAD_DIM)
    queries = queries.reshape(QN, HEAD_DIM)
    query_pos = query_positions(numbers, run).T[0:1, :]
    best = jnp.full((8, QN), FLOOR, f32)
    for core in range(2):
        key_pos = key_positions(kv_ref[core, 2 * KN : 2 * KN + PEERS, :].astype(f32), chunk)
        for n in range(KN // STEP):
            rows = slice(n * STEP, (n + 1) * STEP)
            scores = lax.dot_general(
                kv_ref[core, rows, :], queries, (((1,), (1,)), ((), ())), preferred_element_type=f32
            )
            spread = jnp.concatenate([key_pos[rows, :]] * (QN // HEAD_DIM), axis=1)
            scores = jnp.where(spread <= query_pos, scores * scale, f32(MASKED))
            s_ref[core * KN + n * STEP : core * KN + (n + 1) * STEP, :] = scores
            best = jnp.maximum(best, jnp.max(scores.reshape(STEP // 8, 8, QN), axis=0))
    best = jnp.max(best, axis=0, keepdims=True)
    total = jnp.zeros((8, QN), f32)
    acc = jnp.zeros((HEAD_DIM, QN), f32)
    for core in range(2):
        for n in range(KN // STEP):
            weights = jnp.exp2(s_ref[core * KN + n * STEP : core * KN + (n + 1) * STEP, :] - best)
            total = total + jnp.sum(weights.reshape(STEP // 8, 8, QN), axis=0)
            acc = acc + lax.dot_general(
                kv_ref[core, KN + n * STEP : KN + (n + 1) * STEP, :],
                weights.astype(bf16),
                (((0,), (0,)), ((), ())),
                preferred_element_type=f32,
            )
    total = jnp.sum(total, axis=0, keepdims=True)
    total = jnp.maximum(total, f32(1e-30))
    result = (acc * (1.0 / total)).T
    level = best + jnp.log(total) * math.log2(math.e)
    tiles = QN // 128
    level = jnp.concatenate([level[:, t * 128 : (t + 1) * 128] for t in range(tiles)], axis=0)
    parts = three_parts(level)
    lane = iota((tiles, 128), 1)
    row = iota((TILE, HEAD_DIM), 0)
    for slot in range(128 // TILE):
        shifts = [TILE * (n - slot) % 128 for n in range(3)]
        rolled = [pltpu.roll(x, s, 1) if s else x for x, s in zip(parts, shifts)]
        packed = jnp.where(lane < TILE, rolled[0], jnp.where(lane < 2 * TILE, rolled[1], rolled[2]))
        packed = jnp.where(lane < 3 * TILE, packed, f32(0))
        for t in range(tiles):
            block = t * (128 // TILE) + slot
            mine = result[block * TILE : (block + 1) * TILE, :]
            out_ref[block, :, :] = jnp.where(row < RUN, mine, packed[t : t + 1, :]).astype(bf16)


def finish(part_ref, w_ref, e_ref, out_ref):
    levels = part_ref[...].astype(f32)[:, RUN:TILE, :].reshape(PEERS, HEAD_DIM)
    levels = levels + pltpu.roll(levels, 128 - TILE, 1) + pltpu.roll(levels, 128 - 2 * TILE, 1)
    levels = levels.reshape(RUNS, CHUNKS, HEADS_HERE, 128)
    levels = jnp.exp2(levels - jnp.max(levels, axis=1, keepdims=True))
    shares = levels / jnp.sum(levels, axis=1, keepdims=True)
    shares = jnp.concatenate(
        [shares.reshape(PEERS, 128), jnp.zeros((128 - PEERS, 128), f32)], axis=0
    ).T
    real = iota((TILE, HEAD_DIM), 0) < RUN
    per_slot = SLOT_D // HEAD_DIM
    rows = []
    for u in range(2):
        for i in range(RUNS):
            heads = []
            for h in range(u * per_slot, (u + 1) * per_slot):
                acc = jnp.zeros((TILE, HEAD_DIM), f32)
                for j in range(CHUNKS):
                    block = (i * CHUNKS + j) * HEADS_HERE + h
                    acc = acc + shares[0:TILE, block : block + 1] * part_ref[block, :, :].astype(f32)
                heads.append(jnp.where(real, acc, f32(0)).astype(bf16))
            rows.append(jnp.concatenate(heads, axis=1))
    slots = jnp.concatenate(rows, axis=0)
    embed = jnp.concatenate([e_ref[part, :, :] for part in range(LOCS)], axis=1).astype(f32)
    gain = embed[RUN : RUN + 1, :] + embed[TILE + RUN : TILE + RUN + 1, :] + embed[PAD + RUN : PAD + RUN + 1, :]
    mixed = jnp.dot(slots, w_ref[...], preferred_element_type=f32) + embed
    spread = jnp.sum(mixed * mixed, axis=1, keepdims=True) / LOCAL_D + 1e-05
    normed = (mixed / jnp.sqrt(spread) * gain).astype(bf16)
    for part in range(LOCS):
        out_ref[part, :, :] = normed[:, part * COLS : (part + 1) * COLS]


def unpack(in_ref, out_ref):
    height, rows = LOCS * 2 * PAD, ROWS * PATCH
    to, source = iota((rows, height), 0), iota((rows, height), 1)
    patch = to // PATCH
    row = to % PATCH * PAD + patch // RUN * TILE + patch % RUN
    moved = pick(source == row, in_ref[...].reshape(height, COLS))
    out_ref[...] = moved.astype(bf16)


def vmem(count):
    return [pl.BlockSpec(memory_space=pltpu.VMEM)] * count


def call(kernel, outs, specs, scratch=(), flops=0, moved=0):
    return pl.pallas_call(
        kernel,
        out_shape=outs,
        in_specs=specs,
        out_specs=jax.tree.map(lambda _: pl.BlockSpec(memory_space=pltpu.VMEM), outs),
        scratch_shapes=scratch,
        compiler_params=pltpu.CompilerParams(vmem_limit_bytes=40 * 1024 * 1024),
        cost_estimate=pl.CostEstimate(flops=flops, bytes_accessed=moved, transcendentals=0),
        name=kernel.__name__,
    )


def shape(*dims):
    return jax.ShapeDtypeStruct(dims, bf16)


def on_device(queries, keys, values, positions, byte_embed, w_slot, gain):
    wide = (ROWS, HEADS_HERE * HEAD_DIM)
    sent, embed = call(
        pack,
        [shape(PEERS, 2 * TILE, HEAD_DIM), shape(LOCS, 2 * PAD, COLS)],
        [pl.BlockSpec(memory_space=pl.ANY)] * 6,
        [
            pltpu.SMEM((ROWS,), jnp.int32),
            pltpu.VMEM(wide, bf16),
            pltpu.VMEM(wide, bf16),
            pltpu.VMEM(wide, bf16),
            pltpu.VMEM((ROWS * PATCH, COLS), bf16),
            pltpu.VMEM((1, COLS), f32),
            pltpu.SemaphoreType.DMA((6,)),
        ],
    )(positions, queries, keys, values, byte_embed, gain.reshape(1, COLS))
    held = lax.all_to_all(sent, GROUP, split_axis=0, concat_axis=0, tiled=True)
    embed = lax.all_to_all(embed, "loc", split_axis=0, concat_axis=0, tiled=True)
    kv = call(split, shape(2 * KN + PEERS, HEAD_DIM), vmem(1))(held)
    kv = lax.all_gather(kv, "c", axis=0, tiled=False)
    partial = call(
        attend,
        shape(PEERS, TILE, HEAD_DIM),
        vmem(2),
        [pltpu.VMEM((2 * KN, QN), f32)],
        flops=4 * QN * 2 * KN * HEAD_DIM,
        moved=2 * 4 * KN * HEAD_DIM,
    )(held, kv)
    partial, embed = lax.optimization_barrier((partial, embed))
    partial = lax.all_to_all(partial, GROUP, split_axis=0, concat_axis=0, tiled=True)
    normed = call(finish, shape(LOCS, 2 * PAD, COLS), vmem(3))(partial, w_slot, embed)
    columns = lax.all_to_all(normed, "loc", split_axis=0, concat_axis=0, tiled=True)
    return call(unpack, shape(ROWS * PATCH, COLS), vmem(1))(columns)


def solution(mesh):
    devices = mesh.devices.reshape(2, 2, 2, 4, 2, 2, LOCS)
    finer = Mesh(devices, SEQ + ("loc",))
    placed = (
        P(SEQ, "loc"),
        P(SEQ, "loc"),
        P(SEQ, "loc"),
        P(SEQ),
        P(SEQ, "loc"),
        P(),
        P("loc"),
    )
    return jax.shard_map(
        on_device, mesh=finer, in_specs=placed, out_specs=P(SEQ, "loc"), check_vma=False
    )
```

time: 2170 us -> 85.2 us (0.04)
  the two profiles are of different devices: /device:TPU:16 before, /device:TPU:6 now
where the time goes in v1:
time: 85.2 us; the launch traced here: 83.5 us
  blocking collectives  62.9 us (74%)
  starting transfers between devices  6.2 us (7%)
  Pallas kernels  5.61 us (7%)
  waiting for transfers between devices  4.68 us (5%)
  local copies, waits for them, and re-layouts  4.1 us (5%)
    all_to_all x1, blocking collectives, on_device(): held = lax.all_to_all(sent, GROUP, split_axis=0, concat_axis=0, tiled=True)  31.3 us
    all_to_all x1, blocking collectives, on_device(): lax.all_to_all(partial, GROUP, split_axis=0, concat_axis=0, tiled=True)  16 us
    all_to_all x1, blocking collectives, on_device(): lax.all_to_all(normed, 'loc', split_axis=0, concat_axis=0, tiled=True)  13.4 us
    all_to_all x1, starting transfers between devices, on_device(): lax.all_to_all(embed, 'loc', split_axis=0, concat_axis=0, tiled=True)  6.2 us
    all_to_all x1, waiting for transfers between devices, on_device(): lax.all_to_all(embed, 'loc', split_axis=0, concat_axis=0, tiled=True)  4.68 us
    unnamed x14, local copies, waits for them, and re-layouts  4.1 us
    all_gather x1, blocking collectives, on_device(): kv = lax.all_gather(kv, 'c', axis=0, tiled=False)  2.2 us
    pallas_call x1, Pallas kernels, on_device(): call(attend, shape(PEERS, TILE, HEAD_DIM), vmem(2), [pltpu.VMEM((2 * KN,...  2.11 us
  transfers between devices with their start and end apart: 1, of which 1 were waited for; matrix products, arithmetic and copies ran while one was open for 0% of the time, Pallas kernels for 3%

profile of v1, /device:TPU:6, one launch (start us, length us, event | category | flops | bytes accessed | tf_op | source)
XLA Modules:
  0.0 83.5 jit_solution(14398725155983384595)
XLA Ops:
  0.0 0.0 copy-start.5
  0.0 0.0 copy-start.6
  0.0 0.7 copy-done.5
  0.7 0.0 copy-done.6
  0.7 0.0 copy-start.1
  0.7 0.9 %copy-done.1 = bf16[240,256]{1,0:T(8,128)(2,1)S(1)} copy-done((bf16[240,256]{1,0:T(8,128)(2,1)S(1)}, bf16[240,256]{1,0:T(8,128)(2,1)}, u32[]{:S(2)}) %copy-start.1) | copy-done | bytes 122904
  1.6 0.0 copy-start.2
  1.6 0.8 %copy-done.2 = bf16[30,1024]{1,0:T(8,128)(2,1)S(1)} copy-done((bf16[30,1024]{1,0:T(8,128)(2,1)S(1)}, bf16[30,1024]{1,0:T(8,128)(2,1)}, u32[]{:S(2)}) %copy-start.2) | copy-done | bytes 61464
  2.4 0.0 copy-start.3
  2.4 0.8 %copy-done.3 = bf16[30,1024]{1,0:T(8,128)(2,1)S(1)} copy-done((bf16[30,1024]{1,0:T(8,128)(2,1)S(1)}, bf16[30,1024]{1,0:T(8,128)(2,1)}, u32[]{:S(2)}) %copy-start.3) | copy-done | bytes 61464
  3.3 0.0 copy-start.4
  3.3 0.8 %copy-done.4 = bf16[30,1024]{1,0:T(8,128)(2,1)S(1)} copy-done((bf16[30,1024]{1,0:T(8,128)(2,1)S(1)}, bf16[30,1024]{1,0:T(8,128)(2,1)}, u32[]{:S(2)}) %copy-start.4) | copy-done | bytes 61464
  4.1 1.8 %pack.1 = (bf16[64,32,128]{2,1,0:T(8,128)(2,1)S(1)}, bf16[4,64,256]{2,1,0:T(8,128)(2,1)}) custom-call(s32[30]{0:T(128)S(1)} %copy-done.6, bf16[30,1024]{1,0:T(8,128)(2,1)S(1)} %copy-done.2, bf16[30,1024]{1,0:T(8,128)(2,1)S(1)} %copy-done.3, bf16[30,1024]{1,0:T(8,128)(2,1)S(1)} %copy-done.4, bf16[240,256]{1,0:T(8,128)(2,1)S(1)} %copy-done.1, f32[1,256]{1,0:T(1,128)S(1)} %bitcast.3), custom_call_target="tpu_custom_call" | custom-call | tf_op jit(solution)/shard_map/pack/pallas_call | solution.py:261
  5.9 31.3 %all_to_all.20.in_ref = bf16[64,32,128]{2,1,0:T(8,128)(2,1)S(1)} all-to-all(bf16[64,32,128]{2,1,0:T(8,128)(2,1)S(1)} %get-tuple-element.9), channel_id=1, replica_groups=mesh['za'=2,'zb'=2,'zc'=2,'x'=4,'yl'=2,'c'=2,'loc'=4] {'za','zb','zc','x..., dimensions={0} | all-to-all | bytes 1048576 | tf_op jit(solution)/shard_map/all_to_all | solution.py:275
  37.2 6.2 %all-to-all-start.1 = ((bf16[4,64,256]{2,1,0:T(8,128)(2,1)}), bf16[4,64,256]{2,1,0:T(8,128)(2,1)S(1)}, u32[]{:S(2)}, u32[]{:S(2)}) async-start(bf16[4,64,256]{2,1,0:T(8,128)(2,1)} %get-tuple-element.10), calls=%async_computation.1 | async-start | bytes 262144 | tf_op jit(solution)/shard_map/all_to_all | solution.py:276
  43.4 0.1 split.1
  43.5 2.2 %all-gather = bf16[2176,128]{1,0:T(8,128)(2,1)S(1)} all-gather(bf16[1088,128]{1,0:T(8,128)(2,1)S(1)} %split.1), channel_id=2, replica_groups=mesh['za'=2,'zb'=2,'zc'=2,'x'=4,'yl'=2,'c'=2,'loc'=4] {'c'}, dimensions={0}, use_global_device_ids=true | all-gather | bytes 835584 | tf_op jit(solution)/shard_map/all_gather | solution.py:278
  45.7 0.0 copy-start
  45.7 2.1 %attend.1 = bf16[64,16,128]{2,1,0:T(8,128)(2,1)S(1)} custom-call(bf16[64,32,128]{2,1,0:T(8,128)(2,1)S(1)} %all_to_all.20.in_ref, bf16[2,1088,128]{2,1,0:T(8,128)(2,1)S(1)} %bitcast.2), custom_call_target="tpu_custom_call" | custom-call | flops 536870912 | bytes 524288 | tf_op jit(solution)/shard_map/attend/pallas_call | solution.py:279
  47.8 4.7 %all-to-all-done.1.e_ref = bf16[4,64,256]{2,1,0:T(8,128)(2,1)S(1)} async-done(((bf16[4,64,256]{2,1,0:T(8,128)(2,1)}), bf16[4,64,256]{2,1,0:T(8,128)(2,1)S(1)}, u32[]{:S(2)}, u32[]{:S(2)}) %all-to-all-start.1) | async-done | bytes 131104 | tf_op jit(solution)/shard_map/all_to_all | solution.py:276
  52.5 16.0 %all_to_all.21.part_ref = bf16[64,16,128]{2,1,0:T(8,128)(2,1)S(1)} all-to-all(bf16[64,16,128]{2,1,0:T(8,128)(2,1)S(1)} %attend.1), channel_id=1, replica_groups=mesh['za'=2,'zb'=2,'zc'=2,'x'=4,'yl'=2,'c'=2,'loc'=4] {'za','zb','zc','x..., dimensions={0} | all-to-all | bytes 524288 | tf_op jit(solution)/shard_map/all_to_all | solution.py:288
  68.5 0.0 copy-done
  68.5 0.8 finish.1
  69.3 13.4 %all_to_all.22.in_ref = bf16[4,64,256]{2,1,0:T(8,128)(2,1)S(1)} all-to-all(bf16[4,64,256]{2,1,0:T(8,128)(2,1)S(1)} %finish.1), channel_id=1, replica_groups=mesh['za'=2,'zb'=2,'zc'=2,'x'=4,'yl'=2,'c'=2,'loc'=4] {'loc'}, dimensions={0} | all-to-all | bytes 262144 | tf_op jit(solution)/shard_map/all_to_all | solution.py:290
  82.7 0.9 %unpack.1 = bf16[240,256]{1,0:T(8,128)(2,1)} custom-call(bf16[4,64,256]{2,1,0:T(8,128)(2,1)S(1)} %all_to_all.22.in_ref), custom_call_target="tpu_custom_call" | custom-call | tf_op jit(solution)/shard_map/unpack/pallas_call | solution.py:291
Async XLA Ops:
  0.0 0.7 copy-start.5
  0.0 0.7 copy-start.6
  0.7 0.9 %copy-start.1 = (bf16[240,256]{1,0:T(8,128)(2,1)S(1)}, bf16[240,256]{1,0:T(8,128)(2,1)}, u32[]{:S(2)}) copy-start(bf16[240,256]{1,0:T(8,128)(2,1)} %e_hbm.1) | copy-start | bytes 368644
  1.6 0.8 %copy-start.2 = (bf16[30,1024]{1,0:T(8,128)(2,1)S(1)}, bf16[30,1024]{1,0:T(8,128)(2,1)}, u32[]{:S(2)}) copy-start(bf16[30,1024]{1,0:T(8,128)(2,1)} %q_hbm.1) | copy-start | bytes 184324
  2.4 0.8 %copy-start.3 = (bf16[30,1024]{1,0:T(8,128)(2,1)S(1)}, bf16[30,1024]{1,0:T(8,128)(2,1)}, u32[]{:S(2)}) copy-start(bf16[30,1024]{1,0:T(8,128)(2,1)} %k_hbm.1) | copy-start | bytes 184324
  3.3 0.8 %copy-start.4 = (bf16[30,1024]{1,0:T(8,128)(2,1)S(1)}, bf16[30,1024]{1,0:T(8,128)(2,1)}, u32[]{:S(2)}) copy-start(bf16[30,1024]{1,0:T(8,128)(2,1)} %v_hbm.1) | copy-start | bytes 184324
  37.2 15.3 %all-to-all-start.1 = ((bf16[4,64,256]{2,1,0:T(8,128)(2,1)}), bf16[4,64,256]{2,1,0:T(8,128)(2,1)S(1)}, u32[]{:S(2)}, u32[]{:S(2)}) async-start(bf16[4,64,256]{2,1,0:T(8,128)(2,1)} %get-tuple-element.10), calls=%async_computation.1 | async-start | bytes 262144 | tf_op jit(solution)/shard_map/all_to_all | solution.py:276
  45.7 22.8 %copy-start = (bf16[512,1024]{1,0:T(8,128)(2,1)S(1)}, bf16[512,1024]{1,0:T(8,128)(2,1)}, u32[]{:S(2)}) copy-start(bf16[512,1024]{1,0:T(8,128)(2,1)} %w_ref.1) | copy-start | bytes 3145732

commit v2 on v1

--- a/solution.py
+++ b/solution.py
@@ -51,7 +51,24 @@
 
 
 def pack(
-    pos_hbm, q_hbm, k_hbm, v_hbm, e_hbm, gain_hbm, out_ref, e_out, pos_ref, q_ref, k_ref, v_ref, e_ref, gain_ref, sems
+    pos_hbm,
+    q_hbm,
+    k_hbm,
+    v_hbm,
+    e_hbm,
+    gain_hbm,
+    out_ref,
+    own_out,
+    next_out,
+    across_out,
+    last_out,
+    pos_ref,
+    q_ref,
+    k_ref,
+    v_ref,
+    e_ref,
+    gain_ref,
+    sems,
 ):
     pairs = [
         (pos_hbm, pos_ref),
@@ -96,13 +113,17 @@
     to, source = iota((height, rows), 0), iota((height, rows), 1)
     place = to % TILE
     patch = to // TILE % RUNS * RUN + place
-    moved = pick((source == patch * PATCH + to // PAD) & (place < RUN), e_ref[...])
+    target = (to // (2 * PAD) + lax.axis_index("loc")) % LOCS
+    slot = target * 2 + to // PAD % 2
+    moved = pick((source == patch * PATCH + slot) & (place < RUN), e_ref[...])
     high, middle, low = three_parts(gain_ref[...])
     row = iota((height, COLS), 0) % (2 * PAD)
     moved = jnp.where(row == RUN, high, moved)
     moved = jnp.where(row == TILE + RUN, middle, moved)
     moved = jnp.where(row == PAD + RUN, low, moved)
-    e_out[...] = moved.astype(bf16).reshape(LOCS, 2 * PAD, COLS)
+    moved = moved.astype(bf16)
+    for step, ref in enumerate((own_out, next_out, across_out, last_out)):
+        ref[...] = moved[step * 2 * PAD : (step + 1) * 2 * PAD, :]
 
 
 def split(in_ref, out_ref):
@@ -194,7 +215,10 @@
             out_ref[block, :, :] = jnp.where(row < RUN, mine, packed[t : t + 1, :]).astype(bf16)
 
 
-def finish(part_ref, w_ref, e_ref, out_ref):
+def finish(part_ref, w_ref, own_ref, next_ref, across_ref, last_ref, out_ref, e_ref):
+    for step, ref in enumerate((own_ref, next_ref, across_ref, last_ref)):
+        origin = (lax.axis_index("loc") + LOCS - step) % LOCS
+        e_ref[:, pl.ds(pl.multiple_of(origin * COLS, COLS), COLS)] = ref[...]
     levels = part_ref[...].astype(f32)[:, RUN:TILE, :].reshape(PEERS, HEAD_DIM)
     levels = levels + pltpu.roll(levels, 128 - TILE, 1) + pltpu.roll(levels, 128 - 2 * TILE, 1)
     levels = levels.reshape(RUNS, CHUNKS, HEADS_HERE, 128)
@@ -217,7 +241,7 @@
                 heads.append(jnp.where(real, acc, f32(0)).astype(bf16))
             rows.append(jnp.concatenate(heads, axis=1))
     slots = jnp.concatenate(rows, axis=0)
-    embed = jnp.concatenate([e_ref[part, :, :] for part in range(LOCS)], axis=1).astype(f32)
+    embed = e_ref[...].astype(f32)
     gain = embed[RUN : RUN + 1, :] + embed[TILE + RUN : TILE + RUN + 1, :] + embed[PAD + RUN : PAD + RUN + 1, :]
     mixed = jnp.dot(slots, w_ref[...], preferred_element_type=f32) + embed
     spread = jnp.sum(mixed * mixed, axis=1, keepdims=True) / LOCAL_D + 1e-05
@@ -239,14 +263,14 @@
     return [pl.BlockSpec(memory_space=pltpu.VMEM)] * count
 
 
-def call(kernel, outs, specs, scratch=(), flops=0, moved=0):
+def call(kernel, outs, specs, scratch=(), flops=0, moved=0, limit=40 * 1024 * 1024):
     return pl.pallas_call(
         kernel,
         out_shape=outs,
         in_specs=specs,
         out_specs=jax.tree.map(lambda _: pl.BlockSpec(memory_space=pltpu.VMEM), outs),
         scratch_shapes=scratch,
-        compiler_params=pltpu.CompilerParams(vmem_limit_bytes=40 * 1024 * 1024),
+        compiler_params=pltpu.CompilerParams(vmem_limit_bytes=limit),
         cost_estimate=pl.CostEstimate(flops=flops, bytes_accessed=moved, transcendentals=0),
         name=kernel.__name__,
     )
@@ -256,12 +280,16 @@
     return jax.ShapeDtypeStruct(dims, bf16)
 
 
+def along(block, steps):
+    return lax.ppermute(block, "loc", [(i, (i + steps) % LOCS) for i in range(LOCS)])
+
+
 def on_device(queries, keys, values, positions, byte_embed, w_slot, gain):
     wide = (ROWS, HEADS_HERE * HEAD_DIM)
-    sent, embed = call(
+    sent, *embed = call(
         pack,
-        [shape(PEERS, 2 * TILE, HEAD_DIM), shape(LOCS, 2 * PAD, COLS)],
-        [pl.BlockSpec(memory_space=pl.ANY)] * 6,
+        [shape(PEERS, 2 * TILE, HEAD_DIM)] + [shape(2 * PAD, COLS)] * LOCS,
+        [pl.BlockSpec(memory_space=pltpu.HBM)] * 6,
         [
             pltpu.SMEM((ROWS,), jnp.int32),
             pltpu.VMEM(wide, bf16),
@@ -271,9 +299,12 @@
             pltpu.VMEM((1, COLS), f32),
             pltpu.SemaphoreType.DMA((6,)),
         ],
+        limit=None,
     )(positions, queries, keys, values, byte_embed, gain.reshape(1, COLS))
     held = lax.all_to_all(sent, GROUP, split_axis=0, concat_axis=0, tiled=True)
-    embed = lax.all_to_all(embed, "loc", split_axis=0, concat_axis=0, tiled=True)
+    held, step_one, step_two = lax.optimization_barrier(
+        (held, along(embed[1], 1), along(embed[2], 2))
+    )
     kv = call(split, shape(2 * KN + PEERS, HEAD_DIM), vmem(1))(held)
     kv = lax.all_gather(kv, "c", axis=0, tiled=False)
     partial = call(
@@ -284,9 +315,15 @@
         flops=4 * QN * 2 * KN * HEAD_DIM,
         moved=2 * 4 * KN * HEAD_DIM,
     )(held, kv)
-    partial, embed = lax.optimization_barrier((partial, embed))
+    partial, last = lax.optimization_barrier((partial, embed[3]))
+    embed = [embed[0], step_one, step_two, along(last, 3)]
     partial = lax.all_to_all(partial, GROUP, split_axis=0, concat_axis=0, tiled=True)
-    normed = call(finish, shape(LOCS, 2 * PAD, COLS), vmem(3))(partial, w_slot, embed)
+    normed = call(
+        finish,
+        shape(LOCS, 2 * PAD, COLS),
+        vmem(2 + LOCS),
+        [pltpu.VMEM((2 * PAD, LOCAL_D), bf16)],
+    )(partial, w_slot, *embed)
     columns = lax.all_to_all(normed, "loc", split_axis=0, concat_axis=0, tiled=True)
     return call(unpack, shape(ROWS * PATCH, COLS), vmem(1))(columns)
 

time: 85.2 us -> 75.9 us (0.89)
  the two profiles are of different devices: /device:TPU:6 before, /device:TPU:8 now
where the time goes in v2:
time: 75.9 us; the launch traced here: 75.4 us
  starting transfers between devices  36.6 us (48%)
  waiting for transfers between devices  16.7 us (22%)
  blocking collectives  15.3 us (20%)
  Pallas kernels  6.6 us (9%)
    all_to_all x1, starting transfers between devices, on_device(): held = lax.all_to_all(sent, GROUP, split_axis=0, concat_axis=0, tiled=True)  14.9 us
    ppermute x3, starting transfers between devices, along(): lax.ppermute(block, 'loc', [(i, (i + steps) % LOCS) for i in range(LOCS)])  13.3 us
    all_to_all x1, blocking collectives, on_device(): lax.all_to_all(normed, 'loc', split_axis=0, concat_axis=0, tiled=True)  13.1 us
    all_to_all x1, starting transfers between devices, on_device(): lax.all_to_all(partial, GROUP, split_axis=0, concat_axis=0, tiled=True)  8.33 us
    ppermute x3, waiting for transfers between devices, along(): lax.ppermute(block, 'loc', [(i, (i + steps) % LOCS) for i in range(LOCS)])  7.87 us
    all_to_all x1, waiting for transfers between devices, on_device(): lax.all_to_all(partial, GROUP, split_axis=0, concat_axis=0, tiled=True)  5.88 us
    all_to_all x1, waiting for transfers between devices, on_device(): held = lax.all_to_all(sent, GROUP, split_axis=0, concat_axis=0, tiled=True)  3 us
    pallas_call x1, Pallas kernels, on_device(): call(attend, shape(PEERS, TILE, HEAD_DIM), vmem(2), [pltpu.VMEM((2 * KN,...  2.76 us
  transfers between devices with their start and end apart: 5, of which 4 were waited for; matrix products, arithmetic and copies ran while one was open for 0% of the time, Pallas kernels for 0%

profile of v2, /device:TPU:8, one launch (start us, length us, event | category | flops | bytes accessed | tf_op | source)
XLA Modules:
  0.0 75.4 jit_solution(3378297621972982680)
XLA Ops:
  0.0 2.1 %pack.1 = (bf16[64,32,128]{2,1,0:T(8,128)(2,1)}, bf16[64,256]{1,0:T(8,128)(2,1)}, bf16[64,256]{1,0:T(8,128)(2,1)}, bf16[64,256]{1,0:T(8,128)(2,1)}, bf16[64,256]{1,0:T(8,128)(2,1)}) custom-call(s32[30]{0:T(128)} %pos_hbm.1, bf16[30,1024]{1,0:T(8,128)(2,1)} %q_hbm.1, bf16[30,1024]{1,0:T(8,128)(2,1)} %k_hbm.1, bf16[30,1024]{1,0:T(8,128)(2,1)} %v_hbm.1, ...), custom_call_target="tpu_custom_call" | custom-call | tf_op jit(solution)/shard_map/pack/pallas_call | solution.py:289
  2.1 0.0 copy-start.4
  2.1 0.0 copy-start.3
  2.2 14.9 %all-to-all-start = ((bf16[64,32,128]{2,1,0:T(8,128)(2,1)}), bf16[64,32,128]{2,1,0:T(8,128)(2,1)S(1)}, u32[]{:S(2)}, u32[]{:S(2)}) async-start(bf16[64,32,128]{2,1,0:T(8,128)(2,1)} %get-tuple-element.15), calls=%async_computation | async-start | bytes 1048576 | tf_op jit(solution)/shard_map/all_to_all | solution.py:304
  17.1 0.0 copy-done.4
  17.1 4.5 %collective-permute-start = (bf16[64,256]{1,0:T(8,128)(2,1)S(1)}, bf16[64,256]{1,0:T(8,128)(2,1)S(1)}, u32[]{:S(2)}, u32[]{:S(2)}) collective-permute-start(bf16[64,256]{1,0:T(8,128)(2,1)S(1)} %copy-done.4), channel_id=1, source_target_pairs={{0,1},{1,2},{2,3},{3,0},{4,5},{5,6},{6,7},{7,4},{8,9},{9,10},{10,1... | collective-permute-start | bytes 98312 | tf_op jit(solution)/shard_map/ppermute | solution.py:284
  21.6 0.0 copy-done.3
  21.6 5.0 %collective-permute-start.1 = (bf16[64,256]{1,0:T(8,128)(2,1)S(1)}, bf16[64,256]{1,0:T(8,128)(2,1)S(1)}, u32[]{:S(2)}, u32[]{:S(2)}) collective-permute-start(bf16[64,256]{1,0:T(8,128)(2,1)S(1)} %copy-done.3), channel_id=1, source_target_pairs={{0,2},{1,3},{2,0},{3,1},{4,6},{5,7},{6,4},{7,5},{8,10},{9,11},{10,... | collective-permute-start | bytes 98312 | tf_op jit(solution)/shard_map/ppermute | solution.py:284
  26.7 0.0 collective-permute-done.next_ref
  26.7 4.7 %collective-permute-done.1.across_ref = bf16[64,256]{1,0:T(8,128)(2,1)S(1)} collective-permute-done((bf16[64,256]{1,0:T(8,128)(2,1)S(1)}, bf16[64,256]{1,0:T(8,128)(2,1)S(1)}, u32[]{:S(2)}, u32[]{:S(2)}) %collective-permute-start.1) | collective-permute-done | bytes 32800 | tf_op jit(solution)/shard_map/ppermute | solution.py:284
  31.3 3.0 %all-to-all-done.in_ref = bf16[64,32,128]{2,1,0:T(8,128)(2,1)S(1)} async-done(((bf16[64,32,128]{2,1,0:T(8,128)(2,1)}), bf16[64,32,128]{2,1,0:T(8,128)(2,1)S(1)}, u32[]{:S(2)}, u32[]{:S(2)}) %all-to-all-start) | async-done | bytes 524320 | tf_op jit(solution)/shard_map/all_to_all | solution.py:304
  34.3 0.1 split.1
  34.4 2.2 %all-gather = bf16[2176,128]{1,0:T(8,128)(2,1)S(1)} all-gather(bf16[1088,128]{1,0:T(8,128)(2,1)S(1)} %split.1), channel_id=2, replica_groups=mesh['za'=2,'zb'=2,'zc'=2,'x'=4,'yl'=2,'c'=2,'loc'=4] {'c'}, dimensions={0}, use_global_device_ids=true | all-gather | bytes 835584 | tf_op jit(solution)/shard_map/all_gather | solution.py:309
  36.6 0.0 copy-start
  36.6 2.8 %attend.1 = bf16[64,16,128]{2,1,0:T(8,128)(2,1)} custom-call(bf16[64,32,128]{2,1,0:T(8,128)(2,1)S(1)} %all-to-all-done.in_ref, bf16[2,1088,128]{2,1,0:T(8,128)(2,1)S(1)} %bitcast.2), custom_call_target="tpu_custom_call" | custom-call | flops 536870912 | bytes 524288 | tf_op jit(solution)/shard_map/attend/pallas_call | solution.py:310
  39.4 0.0 copy-start.2
  39.4 0.0 copy-start.1
  39.4 8.3 %all-to-all-start.1 = ((bf16[64,16,128]{2,1,0:T(8,128)(2,1)}), bf16[64,16,128]{2,1,0:T(8,128)(2,1)S(1)}, u32[]{:S(2)}, u32[]{:S(2)}) async-start(bf16[64,16,128]{2,1,0:T(8,128)(2,1)} %attend.1), calls=%async_computation.1 | async-start | bytes 524288 | tf_op jit(solution)/shard_map/all_to_all | solution.py:320
  47.7 0.0 copy-done.2
  47.7 3.8 %collective-permute-start.2 = (bf16[64,256]{1,0:T(8,128)(2,1)S(1)}, bf16[64,256]{1,0:T(8,128)(2,1)S(1)}, u32[]{:S(2)}, u32[]{:S(2)}) collective-permute-start(bf16[64,256]{1,0:T(8,128)(2,1)S(1)} %copy-done.2), channel_id=1, source_target_pairs={{0,3},{1,0},{2,1},{3,2},{4,7},{5,4},{6,5},{7,6},{8,11},{9,8},{10,9... | collective-permute-start | bytes 98312 | tf_op jit(solution)/shard_map/ppermute | solution.py:284
  51.6 3.2 %collective-permute-done.2.last_ref = bf16[64,256]{1,0:T(8,128)(2,1)S(1)} collective-permute-done((bf16[64,256]{1,0:T(8,128)(2,1)S(1)}, bf16[64,256]{1,0:T(8,128)(2,1)S(1)}, u32[]{:S(2)}, u32[]{:S(2)}) %collective-permute-start.2) | collective-permute-done | bytes 32800 | tf_op jit(solution)/shard_map/ppermute | solution.py:284
  54.8 5.9 %all-to-all-done.1.part_ref = bf16[64,16,128]{2,1,0:T(8,128)(2,1)S(1)} async-done(((bf16[64,16,128]{2,1,0:T(8,128)(2,1)}), bf16[64,16,128]{2,1,0:T(8,128)(2,1)S(1)}, u32[]{:S(2)}, u32[]{:S(2)}) %all-to-all-start.1) | async-done | bytes 262176 | tf_op jit(solution)/shard_map/all_to_all | solution.py:320
  60.6 0.0 copy-done
  60.6 0.0 copy-done.1
  60.6 0.8 %finish.1 = bf16[4,64,256]{2,1,0:T(8,128)(2,1)S(1)} custom-call(bf16[64,16,128]{2,1,0:T(8,128)(2,1)S(1)} %all-to-all-done.1.part_ref, bf16[512,1024]{1,0:T(8,128)(2,1)S(1)} %copy-done, bf16[64,256]{1,0:T(8,128)(2,1)S(1)} %copy-done.1, bf16[64,256]{1,0:T(8,128)(2,1)S(1)} %collective-permute-done.next_ref, ...), custom_call_target="tpu_custom_call" | custom-call | tf_op jit(solution)/shard_map/finish/pallas_call | solution.py:321
  61.4 13.1 %all_to_all.15.in_ref = bf16[4,64,256]{2,1,0:T(8,128)(2,1)S(1)} all-to-all(bf16[4,64,256]{2,1,0:T(8,128)(2,1)S(1)} %finish.1), channel_id=1, replica_groups=mesh['za'=2,'zb'=2,'zc'=2,'x'=4,'yl'=2,'c'=2,'loc'=4] {'loc'}, dimensions={0} | all-to-all | bytes 262144 | tf_op jit(solution)/shard_map/all_to_all | solution.py:327
  74.5 0.9 %unpack.1 = bf16[240,256]{1,0:T(8,128)(2,1)} custom-call(bf16[4,64,256]{2,1,0:T(8,128)(2,1)S(1)} %all_to_all.15.in_ref), custom_call_target="tpu_custom_call" | custom-call | tf_op jit(solution)/shard_map/unpack/pallas_call | solution.py:328
Async XLA Ops:
  2.1 15.0 %copy-start.4 = (bf16[64,256]{1,0:T(8,128)(2,1)S(1)}, bf16[64,256]{1,0:T(8,128)(2,1)}, u32[]{:S(2)}) copy-start(bf16[64,256]{1,0:T(8,128)(2,1)} %get-tuple-element.16) | copy-start | bytes 98308
  2.1 19.5 %copy-start.3 = (bf16[64,256]{1,0:T(8,128)(2,1)S(1)}, bf16[64,256]{1,0:T(8,128)(2,1)}, u32[]{:S(2)}) copy-start(bf16[64,256]{1,0:T(8,128)(2,1)} %get-tuple-element.17) | copy-start | bytes 98308
  2.2 32.2 %all-to-all-start = ((bf16[64,32,128]{2,1,0:T(8,128)(2,1)}), bf16[64,32,128]{2,1,0:T(8,128)(2,1)S(1)}, u32[]{:S(2)}, u32[]{:S(2)}) async-start(bf16[64,32,128]{2,1,0:T(8,128)(2,1)} %get-tuple-element.15), calls=%async_computation | async-start | bytes 1048576 | tf_op jit(solution)/shard_map/all_to_all | solution.py:304
  17.1 9.6 %collective-permute-start = (bf16[64,256]{1,0:T(8,128)(2,1)S(1)}, bf16[64,256]{1,0:T(8,128)(2,1)S(1)}, u32[]{:S(2)}, u32[]{:S(2)}) collective-permute-start(bf16[64,256]{1,0:T(8,128)(2,1)S(1)} %copy-done.4), channel_id=1, source_target_pairs={{0,1},{1,2},{2,3},{3,0},{4,5},{5,6},{6,7},{7,4},{8,9},{9,10},{10,1... | collective-permute-start | bytes 98312 | tf_op jit(solution)/shard_map/ppermute | solution.py:284
  21.6 9.7 %collective-permute-start.1 = (bf16[64,256]{1,0:T(8,128)(2,1)S(1)}, bf16[64,256]{1,0:T(8,128)(2,1)S(1)}, u32[]{:S(2)}, u32[]{:S(2)}) collective-permute-start(bf16[64,256]{1,0:T(8,128)(2,1)S(1)} %copy-done.3), channel_id=1, source_target_pairs={{0,2},{1,3},{2,0},{3,1},{4,6},{5,7},{6,4},{7,5},{8,10},{9,11},{10,... | collective-permute-start | bytes 98312 | tf_op jit(solution)/shard_map/ppermute | solution.py:284
  36.6 24.0 %copy-start = (bf16[512,1024]{1,0:T(8,128)(2,1)S(1)}, bf16[512,1024]{1,0:T(8,128)(2,1)}, u32[]{:S(2)}) copy-start(bf16[512,1024]{1,0:T(8,128)(2,1)} %w_ref.1) | copy-start | bytes 3145732
  39.4 8.3 %copy-start.2 = (bf16[64,256]{1,0:T(8,128)(2,1)S(1)}, bf16[64,256]{1,0:T(8,128)(2,1)}, u32[]{:S(2)}) copy-start(bf16[64,256]{1,0:T(8,128)(2,1)} %get-tuple-element.24) | copy-start | bytes 98308
  39.4 21.3 %copy-start.1 = (bf16[64,256]{1,0:T(8,128)(2,1)S(1)}, bf16[64,256]{1,0:T(8,128)(2,1)}, u32[]{:S(2)}) copy-start(bf16[64,256]{1,0:T(8,128)(2,1)} %get-tuple-element.21.own_ref) | copy-start | bytes 98308
  39.4 21.2 %all-to-all-start.1 = ((bf16[64,16,128]{2,1,0:T(8,128)(2,1)}), bf16[64,16,128]{2,1,0:T(8,128)(2,1)S(1)}, u32[]{:S(2)}, u32[]{:S(2)}) async-start(bf16[64,16,128]{2,1,0:T(8,128)(2,1)} %attend.1), calls=%async_computation.1 | async-start | bytes 524288 | tf_op jit(solution)/shard_map/all_to_all | solution.py:320
  47.7 7.0 %collective-permute-start.2 = (bf16[64,256]{1,0:T(8,128)(2,1)S(1)}, bf16[64,256]{1,0:T(8,128)(2,1)S(1)}, u32[]{:S(2)}, u32[]{:S(2)}) collective-permute-start(bf16[64,256]{1,0:T(8,128)(2,1)S(1)} %copy-done.2), channel_id=1, source_target_pairs={{0,3},{1,0},{2,1},{3,2},{4,7},{5,4},{6,5},{7,6},{8,11},{9,8},{10,9... | collective-permute-start | bytes 98312 | tf_op jit(solution)/shard_map/ppermute | solution.py:284

commit v3 on v1

v3 whole, which is shorter than its diff:
```python
import math

import jax
import jax.numpy as jnp
from jax import lax
from jax.experimental import pallas as pl
from jax.experimental.pallas import tpu as pltpu
from jax.sharding import Mesh
from jax.sharding import PartitionSpec as P

HEAD_DIM = 128
PATCH = 8
RUN = 15
RUNS = 2
ROWS = RUN * RUNS
TILE = 16
PAD = RUNS * TILE
CHUNK = 8
CHUNKS = 4
HEADS_HERE = 8
LOCAL_D = 1024
SLOT_D = 512
LOCS = 4
COLS = LOCAL_D // LOCS
SEQ = ("za", "zb", "zc", "x", "yl", "c")
EVERY = SEQ + ("loc",)
DEPTH, PLANE = 8, 8
DEPTH_ORDER = (7, 5, 3, 1, 6, 4, 2, 0)
HOME_ORDER = (7, 5, 3, 1, 6, 4, 2, 0)
HOME_PLACE = tuple(HOME_ORDER.index(z) for z in DEPTH_ORDER)
LOC_ORDER = (2, 3, 1, 0)
SHARDS = DEPTH * PLANE * 2
PEERS = RUNS * CHUNKS * HEADS_HERE
QN = PEERS * TILE
KN = PEERS * CHUNK
STEP = 256
FLOOR = -1e20
MASKED = -1e30
FAR = 1e6
bf16 = jnp.bfloat16
f32 = jnp.float32


def iota(shape, dim):
    return lax.broadcasted_iota(jnp.int32, shape, dim)


def pick(condition, rows):
    select = jnp.where(condition, f32(1), f32(0)).astype(bf16)
    return jnp.dot(select, rows, preferred_element_type=f32)


def three_parts(x):
    high = x.astype(bf16).astype(f32)
    middle = (x - high).astype(bf16).astype(f32)
    return high, middle, x - high - middle


def exchange(blocks, groups):
    return lax.all_to_all(
        blocks, EVERY, split_axis=0, concat_axis=0, tiled=True, axis_index_groups=groups
    )


def seq_groups(depth_order):
    return [
        [((z * PLANE + spot) * 2 + core) * LOCS + loc for z in depth_order for spot in range(PLANE)]
        for core in range(2)
        for loc in range(LOCS)
    ]


def loc_groups():
    return [[shard * LOCS + loc for loc in LOC_ORDER] for shard in range(SHARDS)]


def start_all(pairs, sems):
    copies = [pltpu.make_async_copy(a, b, sems.at[n]) for n, (a, b) in enumerate(pairs)]
    for copy in copies:
        copy.start()
    return copies


def pack(pos_hbm, q_hbm, k_hbm, v_hbm, out_hbm, pos_ref, q_ref, k_ref, v_ref, out_ref, sems, out_sems):
    copies = start_all([(pos_hbm, pos_ref), (q_hbm, q_ref), (k_hbm, k_ref), (v_hbm, v_ref)], sems)
    for copy in copies[:2]:
        copy.wait()

    wide = (PAD, HEADS_HERE * HEAD_DIM)
    to, source = iota((PAD, ROWS), 0), iota((PAD, ROWS), 1)
    place = to % TILE
    queries = pick((source == to // TILE * RUN + place) & (place < RUN), q_ref[...])
    first = (pos_ref[0] // RUN).astype(f32)
    second = (pos_ref[RUN] // RUN).astype(f32)
    numbers = jnp.where(iota(wide, 1) % HEAD_DIM < HEAD_DIM // 2, first, second)
    queries = jnp.where(iota(wide, 0) % TILE == RUN, numbers, queries).astype(bf16)

    for copy in copies[2:]:
        copy.wait()
    to, source = iota((CHUNKS * TILE, ROWS), 0), iota((CHUNKS * TILE, ROWS), 1)
    place = to % TILE
    row = to // TILE * CHUNK + place % CHUNK
    both = pick((source == row) & (place < CHUNK), k_ref[...])
    both = (both + pick((source == row) & (place >= CHUNK), v_ref[...])).astype(bf16)
    sent = []
    for z in range(RUNS * CHUNKS):
        i, j = z // CHUNKS, z % CHUNKS
        for h in range(HEADS_HERE):
            cols = slice(h * HEAD_DIM, (h + 1) * HEAD_DIM)
            out_ref[z * HEADS_HERE + h, 0:TILE, :] = queries[i * TILE : (i + 1) * TILE, cols]
            out_ref[z * HEADS_HERE + h, TILE : 2 * TILE, :] = both[j * TILE : (j + 1) * TILE, cols]
        mine = pl.ds(z * HEADS_HERE, HEADS_HERE)
        sent.append(pltpu.make_async_copy(out_ref.at[mine], out_hbm.at[mine], out_sems.at[z]))
        sent[-1].start()
    for copy in sent:
        copy.wait()


def pack_embed(e_ref, gain_ref, own_out, first_out, second_out):
    height, rows = LOCS * 2 * PAD, ROWS * PATCH
    to, source = iota((height, rows), 0), iota((height, rows), 1)
    place = to % TILE
    patch = to // TILE % RUNS * RUN + place
    slot = (to // (2 * PAD) ^ lax.axis_index("loc")) * 2 + to // PAD % 2
    moved = pick((source == patch * PATCH + slot) & (place < RUN), e_ref[...])
    high, middle, low = three_parts(gain_ref[...])
    row = iota((height, COLS), 0) % (2 * PAD)
    moved = jnp.where(row == RUN, high, moved)
    moved = jnp.where(row == TILE + RUN, middle, moved)
    moved = jnp.where(row == PAD + RUN, low, moved).astype(bf16)
    step = [moved[n * 2 * PAD : (n + 1) * 2 * PAD, :] for n in range(LOCS)]
    own_out[...] = step[0]
    first_out[0, :, :] = step[1]
    first_out[1, :, :] = step[3]
    second_out[...] = step[2]


def split(in_ref, out_ref):
    both = in_ref[:, TILE : 2 * TILE, :].astype(f32)
    out_ref[0:KN, :] = both[:, 0:CHUNK, :].reshape(KN, HEAD_DIM).astype(bf16)
    out_ref[KN : 2 * KN, :] = both[:, CHUNK:TILE, :].reshape(KN, HEAD_DIM).astype(bf16)
    numbers = in_ref[:, 0:TILE, :].astype(f32)[:, RUN:TILE, :]
    out_ref[2 * KN : 2 * KN + PEERS, :] = numbers.reshape(PEERS, HEAD_DIM).astype(bf16)


def run_starts(numbers):
    other = pltpu.roll(numbers, HEAD_DIM // 2, 1)
    lower = iota(numbers.shape, 1) < HEAD_DIM // 2
    return jnp.where(lower, numbers, other) * RUN, jnp.where(lower, other, numbers) * RUN


def key_positions(numbers, chunk):
    spot = iota((PEERS, KN), 1) // CHUNK == iota((PEERS, KN), 0)
    spot = jnp.where(spot, f32(1), f32(0)).astype(bf16)
    both = lax.dot_general(
        numbers, spot, (((0,), (0,)), ((), ())), preferred_element_type=f32
    )
    half = HEAD_DIM // 2
    first, second = both[0:8, :] * RUN, both[half : half + 8, :] * RUN
    row = iota((8, KN), 1) % CHUNK + chunk * CHUNK
    place = row.astype(f32)
    pos = jnp.where(row < RUN, first + place, second + (place - RUN))
    return jnp.where(row < ROWS, pos, f32(FAR))[0:1, :]


def attend(in_ref, kv_ref, out_hbm, out_ref, s_ref, sems):
    scale = math.log2(math.e) / math.sqrt(HEAD_DIM)
    run = 1 - lax.axis_index("zc")
    chunk = 3 - (lax.axis_index("za") * 2 + lax.axis_index("zb"))
    key_pos, values = [], []
    for core in range(2):
        key_pos.append(key_positions(kv_ref[core, 2 * KN : 2 * KN + PEERS, :], chunk))
        ones = jnp.ones((KN, HEAD_DIM), bf16)
        values.append(jnp.concatenate([kv_ref[core, KN : 2 * KN, :], ones], axis=1))
    numbers = in_ref[:, 0:TILE, :].astype(f32)[:, RUN:TILE, :].reshape(PEERS, HEAD_DIM)
    first, second = run_starts(numbers)
    start = jnp.where(run == 0, first, second)
    blocks = STEP // TILE
    line = iota((blocks, TILE, HEAD_DIM), 1)
    lane = iota((blocks, TILE, HEAD_DIM), 2)
    own = (lane % TILE == line) & (lane < 3 * TILE)
    side = iota((blocks, HEAD_DIM), 1) // TILE
    copies = KN // HEAD_DIM
    sent = []
    for t in range(QN // STEP):
        tile = slice(t * blocks, (t + 1) * blocks)
        queries = in_ref[tile, 0:TILE, :].reshape(STEP, HEAD_DIM)
        pos = jnp.broadcast_to(start[tile, None, :], line.shape) + line.astype(f32)
        pos = jnp.where(line < RUN, pos, f32(-1)).reshape(STEP, HEAD_DIM)
        pos = jnp.concatenate([pos] * copies, axis=1)
        best = jnp.full((STEP, HEAD_DIM), FLOOR, f32)
        for core in range(2):
            scores = lax.dot_general(
                queries, kv_ref[core, 0:KN, :], (((1,), (1,)), ((), ())), preferred_element_type=f32
            )
            scores = jnp.where(key_pos[core] <= pos, scores * scale, f32(MASKED))
            s_ref[core, :, :] = scores
            for n in range(copies):
                best = jnp.maximum(best, scores[:, n * HEAD_DIM : (n + 1) * HEAD_DIM])
        best = jnp.broadcast_to(jnp.max(best, axis=1, keepdims=True), best.shape)
        wide = jnp.concatenate([best] * copies, axis=1)
        acc = jnp.zeros((STEP, 2 * HEAD_DIM), f32)
        for core in range(2):
            weights = jnp.exp2(s_ref[core, :, :] - wide).astype(bf16)
            acc = acc + jnp.dot(weights, values[core], preferred_element_type=f32)
        total = jnp.maximum(acc[:, HEAD_DIM:], f32(1e-30))
        result = (acc[:, 0:HEAD_DIM] / total).reshape(line.shape)
        best = jnp.sum(jnp.where(own, best.reshape(own.shape), f32(0)), axis=1)
        total = jnp.sum(jnp.where(own, total.reshape(own.shape), f32(0)), axis=1)
        level = best + jnp.log(jnp.maximum(total, f32(1e-30))) * math.log2(math.e)
        high, middle, low = three_parts(level)
        level = jnp.where(side == 0, high, jnp.where(side == 1, middle, low))
        level = jnp.where(side < 3, level, f32(0))
        level = jnp.broadcast_to(level[:, None, :], line.shape)
        out_ref[tile, :, :] = jnp.where(line < RUN, result, level).astype(bf16)
        for depth in range(t * blocks // PLANE, (t + 1) * blocks // PLANE):
            mine = out_ref.at[pl.ds(depth * PLANE, PLANE)]
            home = out_hbm.at[pl.ds(HOME_PLACE[depth] * PLANE, PLANE)]
            sent.append(pltpu.make_async_copy(mine, home, sems.at[depth]))
            sent[-1].start()
    for copy in sent:
        copy.wait()


def finish(part_ref, w_ref, own_ref, first_ref, second_ref, out_ref, e_ref):
    arrived = (own_ref[...], first_ref[0, :, :], second_ref[0, :, :], second_ref[1, :, :])
    for step, block in enumerate(arrived):
        origin = lax.axis_index("loc") ^ step
        e_ref[:, pl.ds(pl.multiple_of(origin * COLS, COLS), COLS)] = block
    levels = part_ref[...].astype(f32)[:, RUN:TILE, :].reshape(PEERS, HEAD_DIM)
    levels = levels + pltpu.roll(levels, 128 - TILE, 1) + pltpu.roll(levels, 128 - 2 * TILE, 1)
    levels = jnp.concatenate(
        [levels[at * PLANE : (at + 1) * PLANE, :] for at in HOME_PLACE], axis=0
    ).reshape(RUNS, CHUNKS, HEADS_HERE, 128)
    levels = jnp.exp2(levels - jnp.max(levels, axis=1, keepdims=True))
    shares = levels / jnp.sum(levels, axis=1, keepdims=True)
    shares = jnp.concatenate(
        [shares.reshape(PEERS, 128), jnp.zeros((128 - PEERS, 128), f32)], axis=0
    ).T
    real = iota((TILE, HEAD_DIM), 0) < RUN
    per_slot = SLOT_D // HEAD_DIM
    rows = []
    for u in range(2):
        for i in range(RUNS):
            heads = []
            for h in range(u * per_slot, (u + 1) * per_slot):
                acc = jnp.zeros((TILE, HEAD_DIM), f32)
                for j in range(CHUNKS):
                    block = (i * CHUNKS + j) * HEADS_HERE + h
                    partial = part_ref[HOME_PLACE[block // PLANE] * PLANE + h, :, :].astype(f32)
                    acc = acc + shares[0:TILE, block : block + 1] * partial
                heads.append(jnp.where(real, acc, f32(0)).astype(bf16))
            rows.append(jnp.concatenate(heads, axis=1))
    slots = jnp.concatenate(rows, axis=0)
    embed = e_ref[...].astype(f32)
    gain = embed[RUN : RUN + 1, :] + embed[TILE + RUN : TILE + RUN + 1, :] + embed[PAD + RUN : PAD + RUN + 1, :]
    mixed = jnp.dot(slots, w_ref[...], preferred_element_type=f32) + embed
    spread = jnp.sum(mixed * mixed, axis=1, keepdims=True) / LOCAL_D + 1e-05
    normed = (mixed / jnp.sqrt(spread) * gain).astype(bf16)
    for part in range(LOCS):
        out_ref[LOC_ORDER.index(part), :, :] = normed[:, part * COLS : (part + 1) * COLS]


def unpack(in_ref, out_ref):
    height, rows = LOCS * 2 * PAD, ROWS * PATCH
    to, source = iota((rows, height), 0), iota((rows, height), 1)
    patch = to // PATCH
    row = to % PATCH * PAD + patch // RUN * TILE + patch % RUN
    arrived = jnp.concatenate([in_ref[LOC_ORDER.index(loc), :, :] for loc in range(LOCS)], axis=0)
    moved = pick(source == row, arrived)
    out_ref[...] = moved.astype(bf16)


def vmem(count):
    return [pl.BlockSpec(memory_space=pltpu.VMEM)] * count


def call(kernel, outs, specs, scratch=(), flops=0, moved=0, limit=40 * 1024 * 1024, to_hbm=False):
    space = pltpu.HBM if to_hbm else pltpu.VMEM
    return pl.pallas_call(
        kernel,
        out_shape=outs,
        in_specs=specs,
        out_specs=jax.tree.map(lambda _: pl.BlockSpec(memory_space=space), outs),
        scratch_shapes=scratch,
        compiler_params=pltpu.CompilerParams(vmem_limit_bytes=limit),
        cost_estimate=pl.CostEstimate(flops=flops, bytes_accessed=moved, transcendentals=0),
        name=kernel.__name__,
    )


def shape(*dims):
    return jax.ShapeDtypeStruct(dims, bf16)


def swapped(block, step):
    return lax.ppermute(block, "loc", [(i, i ^ step) for i in range(LOCS)])


def on_device(queries, keys, values, positions, byte_embed, w_slot, gain):
    wide = (ROWS, HEADS_HERE * HEAD_DIM)
    messages = (PEERS, 2 * TILE, HEAD_DIM)
    results = (PEERS, TILE, HEAD_DIM)
    sent = call(
        pack,
        shape(*messages),
        [pl.BlockSpec(memory_space=pltpu.HBM)] * 4,
        [
            pltpu.SMEM((ROWS,), jnp.int32),
            pltpu.VMEM(wide, bf16),
            pltpu.VMEM(wide, bf16),
            pltpu.VMEM(wide, bf16),
            pltpu.VMEM(messages, bf16),
            pltpu.SemaphoreType.DMA((4,)),
            pltpu.SemaphoreType.DMA((RUNS * CHUNKS,)),
        ],
        limit=None,
        to_hbm=True,
    )(positions, queries, keys, values)
    sent, byte_embed = lax.optimization_barrier((sent, byte_embed))
    held = exchange(sent, seq_groups(DEPTH_ORDER))
    own, first, second = call(
        pack_embed,
        [shape(2 * PAD, COLS), shape(2, 2 * PAD, COLS), shape(2 * PAD, COLS)],
        vmem(2),
    )(byte_embed, gain.reshape(1, COLS))
    held, first = lax.optimization_barrier((held, swapped(first, 1)))
    kv = call(split, shape(2 * KN + PEERS, HEAD_DIM), vmem(1))(held)
    kv = lax.all_gather(kv, "c", axis=0, tiled=False)
    partial = call(
        attend,
        shape(*results),
        vmem(2),
        [
            pltpu.VMEM(results, bf16),
            pltpu.VMEM((2, STEP, KN), f32),
            pltpu.SemaphoreType.DMA((DEPTH,)),
        ],
        flops=4 * QN * 2 * KN * HEAD_DIM,
        moved=2 * 4 * KN * HEAD_DIM,
        to_hbm=True,
    )(held, kv)
    partial, first, second = lax.optimization_barrier((partial, first, second))
    second = swapped(jnp.stack([second, first[1]]), 2)
    partial = exchange(partial, seq_groups(HOME_ORDER))
    normed = call(
        finish,
        shape(LOCS, 2 * PAD, COLS),
        vmem(5),
        [pltpu.VMEM((2 * PAD, LOCAL_D), bf16)],
    )(partial, w_slot, own, first, second)
    columns = exchange(normed, loc_groups())
    return call(unpack, shape(ROWS * PATCH, COLS), vmem(1))(columns)


def solution(mesh):
    devices = mesh.devices.reshape(2, 2, 2, 4, 2, 2, LOCS)
    finer = Mesh(devices, SEQ + ("loc",))
    placed = (
        P(SEQ, "loc"),
        P(SEQ, "loc"),
        P(SEQ, "loc"),
        P(SEQ),
        P(SEQ, "loc"),
        P(),
        P("loc"),
    )
    return jax.shard_map(
        on_device, mesh=finer, in_specs=placed, out_specs=P(SEQ, "loc"), check_vma=False
    )
```

time: 85.2 us -> 69.9 us (0.82); the launches traced: 83.5 us -> 69.5 us
  blocking collectives: 62.9 us -> 13.8 us
  starting transfers between devices: 6.2 us -> 35.1 us
  waiting for transfers between devices: 4.68 us -> 12.9 us
  local copies, waits for them, and re-layouts: 4.1 us -> 0.68 us
  Pallas kernels: 5.61 us -> 6.84 us
    all_to_all x3 -> x1, blocking collectives: 60.7 us -> 11.6 us  [exchange(): lax.all_to_all(blocks, EVERY, split_axis=0, concat_axis=0, tiled=True, ax...]
    all_to_all x1 -> x2, starting transfers between devices: 6.2 us -> 23.8 us  [exchange(): lax.all_to_all(blocks, EVERY, split_axis=0, concat_axis=0, tiled=True, ax...]
    ppermute x0 -> x2, starting transfers between devices: none -> 11.3 us  [swapped(): return lax.ppermute(block, 'loc', [(i, i ^ step) for i in range(LOCS)])]
    ppermute x0 -> x2, waiting for transfers between devices: none -> 6.22 us  [swapped(): return lax.ppermute(block, 'loc', [(i, i ^ step) for i in range(LOCS)])]
    unnamed x14 -> x6, local copies, waits for them, and re-layouts: 4.1 us -> 0.67 us
    all_to_all x1 -> x2, waiting for transfers between devices: 4.68 us -> 6.68 us  [exchange(): lax.all_to_all(blocks, EVERY, split_axis=0, concat_axis=0, tiled=True, ax...]
    pallas_call x3 -> x4, Pallas kernels: 4.67 us -> 5.9 us  [the longest x1 2.83 us: on_device(): call(attend, shape(*results), vmem(2), [pltpu.VMEM(results, bf16), pltpu....]
  transfers between devices with their start and end apart: 1 -> 4, of which waited for: 1 -> 3; matrix products, arithmetic and copies ran while one was open for 0% -> 0% of each run, Pallas kernels for 3% -> 0%
where the time goes in v3:
time: 69.9 us; the launch traced here: 69.5 us
  starting transfers between devices  35.1 us (50%)
  blocking collectives  13.8 us (20%)
  waiting for transfers between devices  12.9 us (18%)
  Pallas kernels  6.84 us (10%)
    all_to_all x2, starting transfers between devices, exchange(): lax.all_to_all(blocks, EVERY, split_axis=0, concat_axis=0, tiled=True, ax...  23.8 us
    all_to_all x1, blocking collectives, exchange(): lax.all_to_all(blocks, EVERY, split_axis=0, concat_axis=0, tiled=True, ax...  11.6 us
    ppermute x2, starting transfers between devices, swapped(): return lax.ppermute(block, 'loc', [(i, i ^ step) for i in range(LOCS)])  11.3 us
    all_to_all x2, waiting for transfers between devices, exchange(): lax.all_to_all(blocks, EVERY, split_axis=0, concat_axis=0, tiled=True, ax...  6.68 us
    ppermute x2, waiting for transfers between devices, swapped(): return lax.ppermute(block, 'loc', [(i, i ^ step) for i in range(LOCS)])  6.22 us
    pallas_call x1, Pallas kernels, on_device(): call(attend, shape(*results), vmem(2), [pltpu.VMEM(results, bf16), pltpu....  2.83 us
    all_gather x1, blocking collectives, on_device(): kv = lax.all_gather(kv, 'c', axis=0, tiled=False)  2.2 us
    pallas_call x1, Pallas kernels, on_device(): call(pack, shape(*messages), [pl.BlockSpec(memory_space=pltpu.HBM)] * 4,...  2.08 us
  transfers between devices with their start and end apart: 4, of which 3 were waited for; matrix products, arithmetic and copies ran while one was open for 0% of the time, Pallas kernels for 0%

profile of v3, /device:TPU:6, one launch (start us, length us, event | category | flops | bytes accessed | tf_op | source)
XLA Modules:
  0.0 69.5 jit_solution(17339863774641727982)
XLA Ops:
  0.0 2.1 %pack.1 = bf16[64,32,128]{2,1,0:T(8,128)(2,1)} custom-call(s32[30]{0:T(128)} %pos_hbm.1, bf16[30,1024]{1,0:T(8,128)(2,1)} %q_hbm.1, bf16[30,1024]{1,0:T(8,128)(2,1)} %k_hbm.1, bf16[30,1024]{1,0:T(8,128)(2,1)} %v_hbm.1), custom_call_target="tpu_custom_call" | custom-call | tf_op jit(solution)/shard_map/pack/pallas_call | solution.py:304
  2.1 0.0 copy-start.1
  2.1 15.3 %all-to-all-start = ((bf16[64,32,128]{2,1,0:T(8,128)(2,1)}), bf16[64,32,128]{2,1,0:T(8,128)(2,1)S(1)}, u32[]{:S(2)}, u32[]{:S(2)}) async-start(bf16[64,32,128]{2,1,0:T(8,128)(2,1)} %pack.1), calls=%async_computation | async-start | bytes 1048576 | tf_op jit(solution)/shard_map/all_to_all | solution.py:60
  17.4 0.0 copy-start.2
  17.4 0.0 copy-done.1
  17.4 0.7 copy-done.2
  18.1 0.2 pack_embed.1
  18.3 4.5 %collective-permute-start = (bf16[2,64,256]{2,1,0:T(8,128)(2,1)S(1)}, bf16[2,64,256]{2,1,0:T(8,128)(2,1)S(1)}, u32[]{:S(2)}, u32[]{:S(2)}) collective-permute-start(bf16[2,64,256]{2,1,0:T(8,128)(2,1)S(1)} %get-tuple-element.17), channel_id=1, source_target_pairs={{0,1},{1,0},{2,3},{3,2},{4,5},{5,4},{6,7},{7,6},{8,9},{9,8},{10,11... | collective-permute-start | bytes 196616 | tf_op jit(solution)/shard_map/ppermute | solution.py:297
  22.8 2.9 %collective-permute-done.first_ref = bf16[2,64,256]{2,1,0:T(8,128)(2,1)S(1)} collective-permute-done((bf16[2,64,256]{2,1,0:T(8,128)(2,1)S(1)}, bf16[2,64,256]{2,1,0:T(8,128)(2,1)S(1)}, u32[]{:S(2)}, u32[]{:S(2)}) %collective-permute-start) | collective-permute-done | bytes 65568 | tf_op jit(solution)/shard_map/ppermute | solution.py:297
  25.7 6.7 %all-to-all-done.in_ref = bf16[64,32,128]{2,1,0:T(8,128)(2,1)S(1)} async-done(((bf16[64,32,128]{2,1,0:T(8,128)(2,1)}), bf16[64,32,128]{2,1,0:T(8,128)(2,1)S(1)}, u32[]{:S(2)}, u32[]{:S(2)}) %all-to-all-start) | async-done | bytes 524320 | tf_op jit(solution)/shard_map/all_to_all | solution.py:60
  32.4 0.1 split.1
  32.4 2.2 %all-gather = bf16[2176,128]{1,0:T(8,128)(2,1)S(1)} all-gather(bf16[1088,128]{1,0:T(8,128)(2,1)S(1)} %split.1), channel_id=2, replica_groups=mesh['za'=2,'zb'=2,'zc'=2,'x'=4,'yl'=2,'c'=2,'loc'=4] {'c'}, dimensions={0}, use_global_device_ids=true | all-gather | bytes 835584 | tf_op jit(solution)/shard_map/all_gather | solution.py:329
  34.6 0.0 copy-start
  34.6 2.8 %attend.1 = bf16[64,16,128]{2,1,0:T(8,128)(2,1)} custom-call(bf16[64,32,128]{2,1,0:T(8,128)(2,1)S(1)} %all-to-all-done.in_ref, bf16[2,1088,128]{2,1,0:T(8,128)(2,1)S(1)} %bitcast.3), custom_call_target="tpu_custom_call" | custom-call | flops 536870912 | bytes 524288 | tf_op jit(solution)/shard_map/attend/pallas_call | solution.py:330
  37.5 8.5 %all-to-all-start.1 = ((bf16[64,16,128]{2,1,0:T(8,128)(2,1)}), bf16[64,16,128]{2,1,0:T(8,128)(2,1)S(1)}, u32[]{:S(2)}, u32[]{:S(2)}) async-start(bf16[64,16,128]{2,1,0:T(8,128)(2,1)} %attend.1), calls=%async_computation.1 | async-start | bytes 524288 | tf_op jit(solution)/shard_map/all_to_all | solution.py:60
  46.0 6.8 %collective-permute-start.1 = (bf16[2,64,256]{2,1,0:T(8,128)(2,1)S(1)}, bf16[2,64,256]{2,1,0:T(8,128)(2,1)S(1)}, u32[]{:S(2)}, u32[]{:S(2)}) collective-permute-start(bf16[2,64,256]{2,1,0:T(8,128)(2,1)S(1)} %pad_maximum_fusion), channel_id=1, source_target_pairs={{0,2},{1,3},{2,0},{3,1},{4,6},{5,7},{6,4},{7,5},{8,10},{9,11},{10,... | collective-permute-start | bytes 196616 | tf_op jit(solution)/shard_map/ppermute | solution.py:297
  52.9 3.3 %collective-permute-done.1.second_ref = bf16[2,64,256]{2,1,0:T(8,128)(2,1)S(1)} collective-permute-done((bf16[2,64,256]{2,1,0:T(8,128)(2,1)S(1)}, bf16[2,64,256]{2,1,0:T(8,128)(2,1)S(1)}, u32[]{:S(2)}, u32[]{:S(2)}) %collective-permute-start.1) | collective-permute-done | bytes 65568 | tf_op jit(solution)/shard_map/ppermute | solution.py:297
  56.2 0.0 all-to-all-done.1.part_ref
  56.2 0.0 copy-done
  56.2 0.8 %finish.1 = bf16[4,64,256]{2,1,0:T(8,128)(2,1)S(1)} custom-call(bf16[64,16,128]{2,1,0:T(8,128)(2,1)S(1)} %all-to-all-done.1.part_ref, bf16[512,1024]{1,0:T(8,128)(2,1)S(1)} %copy-done, bf16[64,256]{1,0:T(8,128)(2,1)S(1)} %get-tuple-element.22.own_ref, bf16[2,64,256]{2,1,0:T(8,128)(2,1)S(1)} %collective-permute-done.first_ref, ...), custom_call_target="tpu_custom_call" | custom-call | tf_op jit(solution)/shard_map/finish/pallas_call | solution.py:346
  57.0 11.6 %all_to_all.15.in_ref = bf16[4,64,256]{2,1,0:T(8,128)(2,1)S(1)} all-to-all(bf16[4,64,256]{2,1,0:T(8,128)(2,1)S(1)} %finish.1), channel_id=1, replica_groups={{2,3,1,0},{6,7,5,4},{10,11,9,8},{14,15,13,12},{18,19,17,16},{22,23,21,2..., dimensions={0} | all-to-all | bytes 262144 | tf_op jit(solution)/shard_map/all_to_all | solution.py:60
  68.6 0.9 %unpack.1 = bf16[240,256]{1,0:T(8,128)(2,1)} custom-call(bf16[4,64,256]{2,1,0:T(8,128)(2,1)S(1)} %all_to_all.15.in_ref), custom_call_target="tpu_custom_call" | custom-call | tf_op jit(solution)/shard_map/unpack/pallas_call | solution.py:353
  (2 shorter events, 0.0 us)
Async XLA Ops:
  2.1 15.3 %copy-start.1 = (bf16[240,256]{1,0:T(8,128)(2,1)S(1)}, bf16[240,256]{1,0:T(8,128)(2,1)}, u32[]{:S(2)}) copy-start(bf16[240,256]{1,0:T(8,128)(2,1)} %e_ref) | copy-start | bytes 368644
  2.1 30.3 %all-to-all-start = ((bf16[64,32,128]{2,1,0:T(8,128)(2,1)}), bf16[64,32,128]{2,1,0:T(8,128)(2,1)S(1)}, u32[]{:S(2)}, u32[]{:S(2)}) async-start(bf16[64,32,128]{2,1,0:T(8,128)(2,1)} %pack.1), calls=%async_computation | async-start | bytes 1048576 | tf_op jit(solution)/shard_map/all_to_all | solution.py:60
  17.4 0.7 copy-start.2
  18.3 7.4 %collective-permute-start = (bf16[2,64,256]{2,1,0:T(8,128)(2,1)S(1)}, bf16[2,64,256]{2,1,0:T(8,128)(2,1)S(1)}, u32[]{:S(2)}, u32[]{:S(2)}) collective-permute-start(bf16[2,64,256]{2,1,0:T(8,128)(2,1)S(1)} %get-tuple-element.17), channel_id=1, source_target_pairs={{0,1},{1,0},{2,3},{3,2},{4,5},{5,4},{6,7},{7,6},{8,9},{9,8},{10,11... | collective-permute-start | bytes 196616 | tf_op jit(solution)/shard_map/ppermute | solution.py:297
  34.6 21.5 %copy-start = (bf16[512,1024]{1,0:T(8,128)(2,1)S(1)}, bf16[512,1024]{1,0:T(8,128)(2,1)}, u32[]{:S(2)}) copy-start(bf16[512,1024]{1,0:T(8,128)(2,1)} %w_ref.1) | copy-start | bytes 3145732
  37.5 18.7 %all-to-all-start.1 = ((bf16[64,16,128]{2,1,0:T(8,128)(2,1)}), bf16[64,16,128]{2,1,0:T(8,128)(2,1)S(1)}, u32[]{:S(2)}, u32[]{:S(2)}) async-start(bf16[64,16,128]{2,1,0:T(8,128)(2,1)} %attend.1), calls=%async_computation.1 | async-start | bytes 524288 | tf_op jit(solution)/shard_map/all_to_all | solution.py:60
  46.0 10.2 %collective-permute-start.1 = (bf16[2,64,256]{2,1,0:T(8,128)(2,1)S(1)}, bf16[2,64,256]{2,1,0:T(8,128)(2,1)S(1)}, u32[]{:S(2)}, u32[]{:S(2)}) collective-permute-start(bf16[2,64,256]{2,1,0:T(8,128)(2,1)S(1)} %pad_maximum_fusion), channel_id=1, source_target_pairs={{0,2},{1,3},{2,0},{3,1},{4,6},{5,7},{6,4},{7,5},{8,10},{9,11},{10,... | collective-permute-start | bytes 196616 | tf_op jit(solution)/shard_map/ppermute | solution.py:297

commit v4 on v3

--- a/solution.py
+++ b/solution.py
@@ -25,8 +25,8 @@
 SEQ = ("za", "zb", "zc", "x", "yl", "c")
 EVERY = SEQ + ("loc",)
 DEPTH, PLANE = 8, 8
-DEPTH_ORDER = (7, 5, 3, 1, 6, 4, 2, 0)
-HOME_ORDER = (7, 5, 3, 1, 6, 4, 2, 0)
+DEPTH_ORDER = (7, 3, 1, 5, 6, 2, 0, 4)
+HOME_ORDER = (7, 3, 1, 5, 6, 2, 0, 4)
 HOME_PLACE = tuple(HOME_ORDER.index(z) for z in DEPTH_ORDER)
 LOC_ORDER = (2, 3, 1, 0)
 SHARDS = DEPTH * PLANE * 2
@@ -130,9 +130,9 @@
     moved = jnp.where(row == PAD + RUN, low, moved).astype(bf16)
     step = [moved[n * 2 * PAD : (n + 1) * 2 * PAD, :] for n in range(LOCS)]
     own_out[...] = step[0]
-    first_out[0, :, :] = step[1]
-    first_out[1, :, :] = step[3]
-    second_out[...] = step[2]
+    first_out[0, :, :] = step[3]
+    first_out[1, :, :] = step[2]
+    second_out[...] = step[1]
 
 
 def split(in_ref, out_ref):
@@ -165,8 +165,9 @@
 
 def attend(in_ref, kv_ref, out_hbm, out_ref, s_ref, sems):
     scale = math.log2(math.e) / math.sqrt(HEAD_DIM)
-    run = 1 - lax.axis_index("zc")
-    chunk = 3 - (lax.axis_index("za") * 2 + lax.axis_index("zb"))
+    z = lax.axis_index("za") * 4 + lax.axis_index("zb") * 2 + lax.axis_index("zc")
+    place = sum(jnp.where(z == there, n, 0) for n, there in enumerate(DEPTH_ORDER))
+    run, chunk = place // CHUNKS, place % CHUNKS
     key_pos, values = [], []
     for core in range(2):
         key_pos.append(key_positions(kv_ref[core, 2 * KN : 2 * KN + PEERS, :], chunk))
@@ -223,7 +224,7 @@
 
 
 def finish(part_ref, w_ref, own_ref, first_ref, second_ref, out_ref, e_ref):
-    arrived = (own_ref[...], first_ref[0, :, :], second_ref[0, :, :], second_ref[1, :, :])
+    arrived = (own_ref[...], second_ref[0, :, :], second_ref[1, :, :], first_ref[0, :, :])
     for step, block in enumerate(arrived):
         origin = lax.axis_index("loc") ^ step
         e_ref[:, pl.ds(pl.multiple_of(origin * COLS, COLS), COLS)] = block
@@ -324,7 +325,7 @@
         [shape(2 * PAD, COLS), shape(2, 2 * PAD, COLS), shape(2 * PAD, COLS)],
         vmem(2),
     )(byte_embed, gain.reshape(1, COLS))
-    held, first = lax.optimization_barrier((held, swapped(first, 1)))
+    held, first = lax.optimization_barrier((held, swapped(first, 3)))
     kv = call(split, shape(2 * KN + PEERS, HEAD_DIM), vmem(1))(held)
     kv = lax.all_gather(kv, "c", axis=0, tiled=False)
     partial = call(
@@ -341,7 +342,7 @@
         to_hbm=True,
     )(held, kv)
     partial, first, second = lax.optimization_barrier((partial, first, second))
-    second = swapped(jnp.stack([second, first[1]]), 2)
+    second = swapped(jnp.stack([second, first[1]]), 1)
     partial = exchange(partial, seq_groups(HOME_ORDER))
     normed = call(
         finish,

time: 69.9 us -> 68.8 us (0.984)
  starting transfers between devices: 35.1 us -> 33.8 us
    ppermute x2, waiting for transfers between devices: 6.22 us -> 7.88 us  [swapped(): return lax.ppermute(block, 'loc', [(i, i ^ step) for i in range(LOCS)])]
    ppermute x2, starting transfers between devices: 11.3 us -> 9.76 us  [swapped(): return lax.ppermute(block, 'loc', [(i, i ^ step) for i in range(LOCS)])]
    all_to_all x2, waiting for transfers between devices: 6.68 us -> 5.42 us  [exchange(): lax.all_to_all(blocks, EVERY, split_axis=0, concat_axis=0, tiled=True, ax...]
  transfers between devices with their start and end apart: 4 -> 4, of which waited for: 3 -> 4; matrix products, arithmetic and copies ran while one was open for 0% -> 0% of each run, Pallas kernels for 0% -> 0%
where the time goes in v4:
time: 68.8 us; the launch traced here: 68.4 us
  starting transfers between devices  33.8 us (49%)
  blocking collectives  13.7 us (20%)
  waiting for transfers between devices  13.3 us (19%)
  Pallas kernels  6.83 us (10%)
    all_to_all x2, starting transfers between devices, exchange(): lax.all_to_all(blocks, EVERY, split_axis=0, concat_axis=0, tiled=True, ax...  24 us
    all_to_all x1, blocking collectives, exchange(): lax.all_to_all(blocks, EVERY, split_axis=0, concat_axis=0, tiled=True, ax...  11.5 us
    ppermute x2, starting transfers between devices, swapped(): return lax.ppermute(block, 'loc', [(i, i ^ step) for i in range(LOCS)])  9.76 us
    ppermute x2, waiting for transfers between devices, swapped(): return lax.ppermute(block, 'loc', [(i, i ^ step) for i in range(LOCS)])  7.88 us
    all_to_all x2, waiting for transfers between devices, exchange(): lax.all_to_all(blocks, EVERY, split_axis=0, concat_axis=0, tiled=True, ax...  5.42 us
    pallas_call x1, Pallas kernels, on_device(): call(attend, shape(*results), vmem(2), [pltpu.VMEM(results, bf16), pltpu....  2.82 us
    all_gather x1, blocking collectives, on_device(): kv = lax.all_gather(kv, 'c', axis=0, tiled=False)  2.2 us
    pallas_call x1, Pallas kernels, on_device(): call(pack, shape(*messages), [pl.BlockSpec(memory_space=pltpu.HBM)] * 4,...  2.08 us
  transfers between devices with their start and end apart: 4, of which 4 were waited for; matrix products, arithmetic and copies ran while one was open for 0% of the time, Pallas kernels for 0%

profile of v4, /device:TPU:6, one launch (start us, length us, event | category | flops | bytes accessed | tf_op | source)
XLA Modules:
  0.0 68.4 jit_solution(5675218530060803007)
XLA Ops:
  0.0 2.1 %pack.1 = bf16[64,32,128]{2,1,0:T(8,128)(2,1)} custom-call(s32[30]{0:T(128)} %pos_hbm.1, bf16[30,1024]{1,0:T(8,128)(2,1)} %q_hbm.1, bf16[30,1024]{1,0:T(8,128)(2,1)} %k_hbm.1, bf16[30,1024]{1,0:T(8,128)(2,1)} %v_hbm.1), custom_call_target="tpu_custom_call" | custom-call | tf_op jit(solution)/shard_map/pack/pallas_call | solution.py:305
  2.1 0.0 copy-start.1
  2.1 15.2 %all-to-all-start = ((bf16[64,32,128]{2,1,0:T(8,128)(2,1)}), bf16[64,32,128]{2,1,0:T(8,128)(2,1)S(1)}, u32[]{:S(2)}, u32[]{:S(2)}) async-start(bf16[64,32,128]{2,1,0:T(8,128)(2,1)} %pack.1), calls=%async_computation | async-start | bytes 1048576 | tf_op jit(solution)/shard_map/all_to_all | solution.py:60
  17.3 0.0 copy-start.2
  17.3 0.0 copy-done.1
  17.3 0.7 copy-done.2
  18.0 0.2 pack_embed.1
  18.2 5.3 %collective-permute-start = (bf16[2,64,256]{2,1,0:T(8,128)(2,1)S(1)}, bf16[2,64,256]{2,1,0:T(8,128)(2,1)S(1)}, u32[]{:S(2)}, u32[]{:S(2)}) collective-permute-start(bf16[2,64,256]{2,1,0:T(8,128)(2,1)S(1)} %get-tuple-element.17), channel_id=1, source_target_pairs={{0,3},{1,2},{2,1},{3,0},{4,7},{5,6},{6,5},{7,4},{8,11},{9,10},{10,... | collective-permute-start | bytes 196616 | tf_op jit(solution)/shard_map/ppermute | solution.py:298
  23.5 4.2 %collective-permute-done.first_ref = bf16[2,64,256]{2,1,0:T(8,128)(2,1)S(1)} collective-permute-done((bf16[2,64,256]{2,1,0:T(8,128)(2,1)S(1)}, bf16[2,64,256]{2,1,0:T(8,128)(2,1)S(1)}, u32[]{:S(2)}, u32[]{:S(2)}) %collective-permute-start) | collective-permute-done | bytes 65568 | tf_op jit(solution)/shard_map/ppermute | solution.py:298
  27.7 4.2 %all-to-all-done.in_ref = bf16[64,32,128]{2,1,0:T(8,128)(2,1)S(1)} async-done(((bf16[64,32,128]{2,1,0:T(8,128)(2,1)}), bf16[64,32,128]{2,1,0:T(8,128)(2,1)S(1)}, u32[]{:S(2)}, u32[]{:S(2)}) %all-to-all-start) | async-done | bytes 524320 | tf_op jit(solution)/shard_map/all_to_all | solution.py:60
  31.9 0.1 split.1
  31.9 2.2 %all-gather = bf16[2176,128]{1,0:T(8,128)(2,1)S(1)} all-gather(bf16[1088,128]{1,0:T(8,128)(2,1)S(1)} %split.1), channel_id=2, replica_groups=mesh['za'=2,'zb'=2,'zc'=2,'x'=4,'yl'=2,'c'=2,'loc'=4] {'c'}, dimensions={0}, use_global_device_ids=true | all-gather | bytes 835584 | tf_op jit(solution)/shard_map/all_gather | solution.py:330
  34.2 0.0 copy-start
  34.2 2.8 %attend.1 = bf16[64,16,128]{2,1,0:T(8,128)(2,1)} custom-call(bf16[64,32,128]{2,1,0:T(8,128)(2,1)S(1)} %all-to-all-done.in_ref, bf16[2,1088,128]{2,1,0:T(8,128)(2,1)S(1)} %bitcast.3), custom_call_target="tpu_custom_call" | custom-call | flops 536870912 | bytes 524288 | tf_op jit(solution)/shard_map/attend/pallas_call | solution.py:331
  37.0 8.8 %all-to-all-start.1 = ((bf16[64,16,128]{2,1,0:T(8,128)(2,1)}), bf16[64,16,128]{2,1,0:T(8,128)(2,1)S(1)}, u32[]{:S(2)}, u32[]{:S(2)}) async-start(bf16[64,16,128]{2,1,0:T(8,128)(2,1)} %attend.1), calls=%async_computation.1 | async-start | bytes 524288 | tf_op jit(solution)/shard_map/all_to_all | solution.py:60
  45.9 4.5 %collective-permute-start.1 = (bf16[2,64,256]{2,1,0:T(8,128)(2,1)S(1)}, bf16[2,64,256]{2,1,0:T(8,128)(2,1)S(1)}, u32[]{:S(2)}, u32[]{:S(2)}) collective-permute-start(bf16[2,64,256]{2,1,0:T(8,128)(2,1)S(1)} %pad_maximum_fusion), channel_id=1, source_target_pairs={{0,1},{1,0},{2,3},{3,2},{4,5},{5,4},{6,7},{7,6},{8,9},{9,8},{10,11... | collective-permute-start | bytes 196616 | tf_op jit(solution)/shard_map/ppermute | solution.py:298
  50.4 3.7 %collective-permute-done.1.second_ref = bf16[2,64,256]{2,1,0:T(8,128)(2,1)S(1)} collective-permute-done((bf16[2,64,256]{2,1,0:T(8,128)(2,1)S(1)}, bf16[2,64,256]{2,1,0:T(8,128)(2,1)S(1)}, u32[]{:S(2)}, u32[]{:S(2)}) %collective-permute-start.1) | collective-permute-done | bytes 65568 | tf_op jit(solution)/shard_map/ppermute | solution.py:298
  54.1 1.2 %all-to-all-done.1.part_ref = bf16[64,16,128]{2,1,0:T(8,128)(2,1)S(1)} async-done(((bf16[64,16,128]{2,1,0:T(8,128)(2,1)}), bf16[64,16,128]{2,1,0:T(8,128)(2,1)S(1)}, u32[]{:S(2)}, u32[]{:S(2)}) %all-to-all-start.1) | async-done | bytes 262176 | tf_op jit(solution)/shard_map/all_to_all | solution.py:60
  55.3 0.0 copy-done
  55.3 0.8 %finish.1 = bf16[4,64,256]{2,1,0:T(8,128)(2,1)S(1)} custom-call(bf16[64,16,128]{2,1,0:T(8,128)(2,1)S(1)} %all-to-all-done.1.part_ref, bf16[512,1024]{1,0:T(8,128)(2,1)S(1)} %copy-done, bf16[64,256]{1,0:T(8,128)(2,1)S(1)} %get-tuple-element.22.own_ref, bf16[2,64,256]{2,1,0:T(8,128)(2,1)S(1)} %collective-permute-done.first_ref, ...), custom_call_target="tpu_custom_call" | custom-call | tf_op jit(solution)/shard_map/finish/pallas_call | solution.py:347
  56.1 11.5 %all_to_all.15.in_ref = bf16[4,64,256]{2,1,0:T(8,128)(2,1)S(1)} all-to-all(bf16[4,64,256]{2,1,0:T(8,128)(2,1)S(1)} %finish.1), channel_id=1, replica_groups={{2,3,1,0},{6,7,5,4},{10,11,9,8},{14,15,13,12},{18,19,17,16},{22,23,21,2..., dimensions={0} | all-to-all | bytes 262144 | tf_op jit(solution)/shard_map/all_to_all | solution.py:60
  67.5 0.9 %unpack.1 = bf16[240,256]{1,0:T(8,128)(2,1)} custom-call(bf16[4,64,256]{2,1,0:T(8,128)(2,1)S(1)} %all_to_all.15.in_ref), custom_call_target="tpu_custom_call" | custom-call | tf_op jit(solution)/shard_map/unpack/pallas_call | solution.py:354
  (2 shorter events, 0.0 us)
Async XLA Ops:
  2.1 15.2 %copy-start.1 = (bf16[240,256]{1,0:T(8,128)(2,1)S(1)}, bf16[240,256]{1,0:T(8,128)(2,1)}, u32[]{:S(2)}) copy-start(bf16[240,256]{1,0:T(8,128)(2,1)} %e_ref) | copy-start | bytes 368644
  2.1 29.8 %all-to-all-start = ((bf16[64,32,128]{2,1,0:T(8,128)(2,1)}), bf16[64,32,128]{2,1,0:T(8,128)(2,1)S(1)}, u32[]{:S(2)}, u32[]{:S(2)}) async-start(bf16[64,32,128]{2,1,0:T(8,128)(2,1)} %pack.1), calls=%async_computation | async-start | bytes 1048576 | tf_op jit(solution)/shard_map/all_to_all | solution.py:60
  17.3 0.7 copy-start.2
  18.2 9.4 %collective-permute-start = (bf16[2,64,256]{2,1,0:T(8,128)(2,1)S(1)}, bf16[2,64,256]{2,1,0:T(8,128)(2,1)S(1)}, u32[]{:S(2)}, u32[]{:S(2)}) collective-permute-start(bf16[2,64,256]{2,1,0:T(8,128)(2,1)S(1)} %get-tuple-element.17), channel_id=1, source_target_pairs={{0,3},{1,2},{2,1},{3,0},{4,7},{5,6},{6,5},{7,4},{8,11},{9,10},{10,... | collective-permute-start | bytes 196616 | tf_op jit(solution)/shard_map/ppermute | solution.py:298
  34.2 21.1 %copy-start = (bf16[512,1024]{1,0:T(8,128)(2,1)S(1)}, bf16[512,1024]{1,0:T(8,128)(2,1)}, u32[]{:S(2)}) copy-start(bf16[512,1024]{1,0:T(8,128)(2,1)} %w_ref.1) | copy-start | bytes 3145732
  37.0 18.3 %all-to-all-start.1 = ((bf16[64,16,128]{2,1,0:T(8,128)(2,1)}), bf16[64,16,128]{2,1,0:T(8,128)(2,1)S(1)}, u32[]{:S(2)}, u32[]{:S(2)}) async-start(bf16[64,16,128]{2,1,0:T(8,128)(2,1)} %attend.1), calls=%async_computation.1 | async-start | bytes 524288 | tf_op jit(solution)/shard_map/all_to_all | solution.py:60
  45.9 8.2 %collective-permute-start.1 = (bf16[2,64,256]{2,1,0:T(8,128)(2,1)S(1)}, bf16[2,64,256]{2,1,0:T(8,128)(2,1)S(1)}, u32[]{:S(2)}, u32[]{:S(2)}) collective-permute-start(bf16[2,64,256]{2,1,0:T(8,128)(2,1)S(1)} %pad_maximum_fusion), channel_id=1, source_target_pairs={{0,1},{1,0},{2,3},{3,2},{4,5},{5,4},{6,7},{7,6},{8,9},{9,8},{10,11... | collective-permute-start | bytes 196616 | tf_op jit(solution)/shard_map/ppermute | solution.py:298

commit v5 on v4

--- a/solution.py
+++ b/solution.py
@@ -26,9 +26,9 @@
 EVERY = SEQ + ("loc",)
 DEPTH, PLANE = 8, 8
 DEPTH_ORDER = (7, 3, 1, 5, 6, 2, 0, 4)
-HOME_ORDER = (7, 3, 1, 5, 6, 2, 0, 4)
+HOME_ORDER = (7, 2, 4, 3, 5, 0, 6, 1)
 HOME_PLACE = tuple(HOME_ORDER.index(z) for z in DEPTH_ORDER)
-LOC_ORDER = (2, 3, 1, 0)
+LOC_ORDER = (2, 0, 1, 3)
 SHARDS = DEPTH * PLANE * 2
 PEERS = RUNS * CHUNKS * HEADS_HERE
 QN = PEERS * TILE

time: 68.8 us -> 68.6 us (level)
  no operation moved by 1% of the time
where the time goes in v5:
time: 68.6 us; the launch traced here: 68.1 us
  starting transfers between devices  33.7 us (49%)
  blocking collectives  13.8 us (20%)
  waiting for transfers between devices  13 us (19%)
  Pallas kernels  6.83 us (10%)
    all_to_all x2, starting transfers between devices, exchange(): lax.all_to_all(blocks, EVERY, split_axis=0, concat_axis=0, tiled=True, ax...  24 us
    all_to_all x1, blocking collectives, exchange(): lax.all_to_all(blocks, EVERY, split_axis=0, concat_axis=0, tiled=True, ax...  11.6 us
    ppermute x2, starting transfers between devices, swapped(): return lax.ppermute(block, 'loc', [(i, i ^ step) for i in range(LOCS)])  9.76 us
    ppermute x2, waiting for transfers between devices, swapped(): return lax.ppermute(block, 'loc', [(i, i ^ step) for i in range(LOCS)])  7.88 us
    all_to_all x2, waiting for transfers between devices, exchange(): lax.all_to_all(blocks, EVERY, split_axis=0, concat_axis=0, tiled=True, ax...  5.07 us
    pallas_call x1, Pallas kernels, on_device(): call(attend, shape(*results), vmem(2), [pltpu.VMEM(results, bf16), pltpu....  2.82 us
    all_gather x1, blocking collectives, on_device(): kv = lax.all_gather(kv, 'c', axis=0, tiled=False)  2.2 us
    pallas_call x1, Pallas kernels, on_device(): call(pack, shape(*messages), [pl.BlockSpec(memory_space=pltpu.HBM)] * 4,...  2.08 us
  transfers between devices with their start and end apart: 4, of which 4 were waited for; matrix products, arithmetic and copies ran while one was open for 0% of the time, Pallas kernels for 0%

profile of v5, /device:TPU:6, one launch (start us, length us, event | category | flops | bytes accessed | tf_op | source)
XLA Modules:
  0.0 68.1 jit_solution(15249291703445350910)
XLA Ops:
  0.0 2.1 %pack.1 = bf16[64,32,128]{2,1,0:T(8,128)(2,1)} custom-call(s32[30]{0:T(128)} %pos_hbm.1, bf16[30,1024]{1,0:T(8,128)(2,1)} %q_hbm.1, bf16[30,1024]{1,0:T(8,128)(2,1)} %k_hbm.1, bf16[30,1024]{1,0:T(8,128)(2,1)} %v_hbm.1), custom_call_target="tpu_custom_call" | custom-call | tf_op jit(solution)/shard_map/pack/pallas_call | solution.py:305
  2.1 0.0 copy-start.1
  2.1 15.2 %all-to-all-start = ((bf16[64,32,128]{2,1,0:T(8,128)(2,1)}), bf16[64,32,128]{2,1,0:T(8,128)(2,1)S(1)}, u32[]{:S(2)}, u32[]{:S(2)}) async-start(bf16[64,32,128]{2,1,0:T(8,128)(2,1)} %pack.1), calls=%async_computation | async-start | bytes 1048576 | tf_op jit(solution)/shard_map/all_to_all | solution.py:60
  17.3 0.0 copy-start.2
  17.3 0.0 copy-done.1
  17.3 0.7 copy-done.2
  18.0 0.2 pack_embed.1
  18.2 5.3 %collective-permute-start = (bf16[2,64,256]{2,1,0:T(8,128)(2,1)S(1)}, bf16[2,64,256]{2,1,0:T(8,128)(2,1)S(1)}, u32[]{:S(2)}, u32[]{:S(2)}) collective-permute-start(bf16[2,64,256]{2,1,0:T(8,128)(2,1)S(1)} %get-tuple-element.17), channel_id=1, source_target_pairs={{0,3},{1,2},{2,1},{3,0},{4,7},{5,6},{6,5},{7,4},{8,11},{9,10},{10,... | collective-permute-start | bytes 196616 | tf_op jit(solution)/shard_map/ppermute | solution.py:298
  23.5 4.2 %collective-permute-done.first_ref = bf16[2,64,256]{2,1,0:T(8,128)(2,1)S(1)} collective-permute-done((bf16[2,64,256]{2,1,0:T(8,128)(2,1)S(1)}, bf16[2,64,256]{2,1,0:T(8,128)(2,1)S(1)}, u32[]{:S(2)}, u32[]{:S(2)}) %collective-permute-start) | collective-permute-done | bytes 65568 | tf_op jit(solution)/shard_map/ppermute | solution.py:298
  27.7 4.2 %all-to-all-done.in_ref = bf16[64,32,128]{2,1,0:T(8,128)(2,1)S(1)} async-done(((bf16[64,32,128]{2,1,0:T(8,128)(2,1)}), bf16[64,32,128]{2,1,0:T(8,128)(2,1)S(1)}, u32[]{:S(2)}, u32[]{:S(2)}) %all-to-all-start) | async-done | bytes 524320 | tf_op jit(solution)/shard_map/all_to_all | solution.py:60
  31.9 0.1 split.1
  31.9 2.2 %all-gather = bf16[2176,128]{1,0:T(8,128)(2,1)S(1)} all-gather(bf16[1088,128]{1,0:T(8,128)(2,1)S(1)} %split.1), channel_id=2, replica_groups=mesh['za'=2,'zb'=2,'zc'=2,'x'=4,'yl'=2,'c'=2,'loc'=4] {'c'}, dimensions={0}, use_global_device_ids=true | all-gather | bytes 835584 | tf_op jit(solution)/shard_map/all_gather | solution.py:330
  34.2 0.0 copy-start
  34.2 2.8 %attend.1 = bf16[64,16,128]{2,1,0:T(8,128)(2,1)} custom-call(bf16[64,32,128]{2,1,0:T(8,128)(2,1)S(1)} %all-to-all-done.in_ref, bf16[2,1088,128]{2,1,0:T(8,128)(2,1)S(1)} %bitcast.3), custom_call_target="tpu_custom_call" | custom-call | flops 536870912 | bytes 524288 | tf_op jit(solution)/shard_map/attend/pallas_call | solution.py:331
  37.0 8.8 %all-to-all-start.1 = ((bf16[64,16,128]{2,1,0:T(8,128)(2,1)}), bf16[64,16,128]{2,1,0:T(8,128)(2,1)S(1)}, u32[]{:S(2)}, u32[]{:S(2)}) async-start(bf16[64,16,128]{2,1,0:T(8,128)(2,1)} %attend.1), calls=%async_computation.1 | async-start | bytes 524288 | tf_op jit(solution)/shard_map/all_to_all | solution.py:60
  45.8 4.5 %collective-permute-start.1 = (bf16[2,64,256]{2,1,0:T(8,128)(2,1)S(1)}, bf16[2,64,256]{2,1,0:T(8,128)(2,1)S(1)}, u32[]{:S(2)}, u32[]{:S(2)}) collective-permute-start(bf16[2,64,256]{2,1,0:T(8,128)(2,1)S(1)} %pad_maximum_fusion), channel_id=1, source_target_pairs={{0,1},{1,0},{2,3},{3,2},{4,5},{5,4},{6,7},{7,6},{8,9},{9,8},{10,11... | collective-permute-start | bytes 196616 | tf_op jit(solution)/shard_map/ppermute | solution.py:298
  50.3 3.7 %collective-permute-done.1.second_ref = bf16[2,64,256]{2,1,0:T(8,128)(2,1)S(1)} collective-permute-done((bf16[2,64,256]{2,1,0:T(8,128)(2,1)S(1)}, bf16[2,64,256]{2,1,0:T(8,128)(2,1)S(1)}, u32[]{:S(2)}, u32[]{:S(2)}) %collective-permute-start.1) | collective-permute-done | bytes 65568 | tf_op jit(solution)/shard_map/ppermute | solution.py:298
  54.0 0.9 %all-to-all-done.1.part_ref = bf16[64,16,128]{2,1,0:T(8,128)(2,1)S(1)} async-done(((bf16[64,16,128]{2,1,0:T(8,128)(2,1)}), bf16[64,16,128]{2,1,0:T(8,128)(2,1)S(1)}, u32[]{:S(2)}, u32[]{:S(2)}) %all-to-all-start.1) | async-done | bytes 262176 | tf_op jit(solution)/shard_map/all_to_all | solution.py:60
  54.9 0.0 copy-done
  54.9 0.8 %finish.1 = bf16[4,64,256]{2,1,0:T(8,128)(2,1)S(1)} custom-call(bf16[64,16,128]{2,1,0:T(8,128)(2,1)S(1)} %all-to-all-done.1.part_ref, bf16[512,1024]{1,0:T(8,128)(2,1)S(1)} %copy-done, bf16[64,256]{1,0:T(8,128)(2,1)S(1)} %get-tuple-element.22.own_ref, bf16[2,64,256]{2,1,0:T(8,128)(2,1)S(1)} %collective-permute-done.first_ref, ...), custom_call_target="tpu_custom_call" | custom-call | tf_op jit(solution)/shard_map/finish/pallas_call | solution.py:347
  55.7 11.6 %all_to_all.15.in_ref = bf16[4,64,256]{2,1,0:T(8,128)(2,1)S(1)} all-to-all(bf16[4,64,256]{2,1,0:T(8,128)(2,1)S(1)} %finish.1), channel_id=1, replica_groups={{2,0,1,3},{6,4,5,7},{10,8,9,11},{14,12,13,15},{18,16,17,19},{22,20,21,2..., dimensions={0} | all-to-all | bytes 262144 | tf_op jit(solution)/shard_map/all_to_all | solution.py:60
  67.2 0.9 %unpack.1 = bf16[240,256]{1,0:T(8,128)(2,1)} custom-call(bf16[4,64,256]{2,1,0:T(8,128)(2,1)S(1)} %all_to_all.15.in_ref), custom_call_target="tpu_custom_call" | custom-call | tf_op jit(solution)/shard_map/unpack/pallas_call | solution.py:354
  (2 shorter events, 0.0 us)
Async XLA Ops:
  2.1 15.2 %copy-start.1 = (bf16[240,256]{1,0:T(8,128)(2,1)S(1)}, bf16[240,256]{1,0:T(8,128)(2,1)}, u32[]{:S(2)}) copy-start(bf16[240,256]{1,0:T(8,128)(2,1)} %e_ref) | copy-start | bytes 368644
  2.1 29.8 %all-to-all-start = ((bf16[64,32,128]{2,1,0:T(8,128)(2,1)}), bf16[64,32,128]{2,1,0:T(8,128)(2,1)S(1)}, u32[]{:S(2)}, u32[]{:S(2)}) async-start(bf16[64,32,128]{2,1,0:T(8,128)(2,1)} %pack.1), calls=%async_computation | async-start | bytes 1048576 | tf_op jit(solution)/shard_map/all_to_all | solution.py:60
  17.3 0.7 %copy-start.2 = (f32[256]{0:T(256)S(1)}, f32[256]{0:T(256)}, u32[]{:S(2)}) copy-start(f32[256]{0:T(256)} %param.13) | copy-start | bytes 3076
  18.2 9.4 %collective-permute-start = (bf16[2,64,256]{2,1,0:T(8,128)(2,1)S(1)}, bf16[2,64,256]{2,1,0:T(8,128)(2,1)S(1)}, u32[]{:S(2)}, u32[]{:S(2)}) collective-permute-start(bf16[2,64,256]{2,1,0:T(8,128)(2,1)S(1)} %get-tuple-element.17), channel_id=1, source_target_pairs={{0,3},{1,2},{2,1},{3,0},{4,7},{5,6},{6,5},{7,4},{8,11},{9,10},{10,... | collective-permute-start | bytes 196616 | tf_op jit(solution)/shard_map/ppermute | solution.py:298
  34.2 20.7 %copy-start = (bf16[512,1024]{1,0:T(8,128)(2,1)S(1)}, bf16[512,1024]{1,0:T(8,128)(2,1)}, u32[]{:S(2)}) copy-start(bf16[512,1024]{1,0:T(8,128)(2,1)} %w_ref.1) | copy-start | bytes 3145732
  37.0 17.9 %all-to-all-start.1 = ((bf16[64,16,128]{2,1,0:T(8,128)(2,1)}), bf16[64,16,128]{2,1,0:T(8,128)(2,1)S(1)}, u32[]{:S(2)}, u32[]{:S(2)}) async-start(bf16[64,16,128]{2,1,0:T(8,128)(2,1)} %attend.1), calls=%async_computation.1 | async-start | bytes 524288 | tf_op jit(solution)/shard_map/all_to_all | solution.py:60
  45.8 8.2 %collective-permute-start.1 = (bf16[2,64,256]{2,1,0:T(8,128)(2,1)S(1)}, bf16[2,64,256]{2,1,0:T(8,128)(2,1)S(1)}, u32[]{:S(2)}, u32[]{:S(2)}) collective-permute-start(bf16[2,64,256]{2,1,0:T(8,128)(2,1)S(1)} %pad_maximum_fusion), channel_id=1, source_target_pairs={{0,1},{1,0},{2,3},{3,2},{4,5},{5,4},{6,7},{7,6},{8,9},{9,8},{10,11... | collective-permute-start | bytes 196616 | tf_op jit(solution)/shard_map/ppermute | solution.py:298

commit v6 on v5

--- a/solution.py
+++ b/solution.py
@@ -45,9 +45,12 @@
     return lax.broadcasted_iota(jnp.int32, shape, dim)
 
 
+def picker(condition):
+    return jnp.where(condition, f32(1), f32(0)).astype(bf16)
+
+
 def pick(condition, rows):
-    select = jnp.where(condition, f32(1), f32(0)).astype(bf16)
-    return jnp.dot(select, rows, preferred_element_type=f32)
+    return jnp.dot(picker(condition), rows, preferred_element_type=f32)
 
 
 def three_parts(x):
@@ -83,25 +86,29 @@
 
 def pack(pos_hbm, q_hbm, k_hbm, v_hbm, out_hbm, pos_ref, q_ref, k_ref, v_ref, out_ref, sems, out_sems):
     copies = start_all([(pos_hbm, pos_ref), (q_hbm, q_ref), (k_hbm, k_ref), (v_hbm, v_ref)], sems)
-    for copy in copies[:2]:
-        copy.wait()
-
     wide = (PAD, HEADS_HERE * HEAD_DIM)
     to, source = iota((PAD, ROWS), 0), iota((PAD, ROWS), 1)
     place = to % TILE
-    queries = pick((source == to // TILE * RUN + place) & (place < RUN), q_ref[...])
-    first = (pos_ref[0] // RUN).astype(f32)
-    second = (pos_ref[RUN] // RUN).astype(f32)
-    numbers = jnp.where(iota(wide, 1) % HEAD_DIM < HEAD_DIM // 2, first, second)
-    queries = jnp.where(iota(wide, 0) % TILE == RUN, numbers, queries).astype(bf16)
-
-    for copy in copies[2:]:
-        copy.wait()
+    pick_queries = picker((source == to // TILE * RUN + place) & (place < RUN))
+    first_half = iota(wide, 1) % HEAD_DIM < HEAD_DIM // 2
+    spare = iota(wide, 0) % TILE == RUN
     to, source = iota((CHUNKS * TILE, ROWS), 0), iota((CHUNKS * TILE, ROWS), 1)
     place = to % TILE
     row = to // TILE * CHUNK + place % CHUNK
-    both = pick((source == row) & (place < CHUNK), k_ref[...])
-    both = (both + pick((source == row) & (place >= CHUNK), v_ref[...])).astype(bf16)
+    pick_keys = picker((source == row) & (place < CHUNK))
+    pick_values = picker((source == row) & (place >= CHUNK))
+
+    for copy in copies[2:]:
+        copy.wait()
+    both = jnp.dot(pick_keys, k_ref[...], preferred_element_type=f32)
+    both = (both + jnp.dot(pick_values, v_ref[...], preferred_element_type=f32)).astype(bf16)
+    for copy in copies[:2]:
+        copy.wait()
+    queries = jnp.dot(pick_queries, q_ref[...], preferred_element_type=f32)
+    first = (pos_ref[0] // RUN).astype(f32)
+    second = (pos_ref[RUN] // RUN).astype(f32)
+    numbers = jnp.where(first_half, first, second)
+    queries = jnp.where(spare, numbers, queries).astype(bf16)
     sent = []
     for z in range(RUNS * CHUNKS):
         i, j = z // CHUNKS, z % CHUNKS

time: 68.6 us -> 68.7 us (level)
  no operation moved by 1% of the time
where the time goes in v6:
time: 68.7 us; the launch traced here: 68.2 us
  starting transfers between devices  33.7 us (49%)
  blocking collectives  13.8 us (20%)
  waiting for transfers between devices  13 us (19%)
  Pallas kernels  6.91 us (10%)
    all_to_all x2, starting transfers between devices, exchange(): lax.all_to_all(blocks, EVERY, split_axis=0, concat_axis=0, tiled=True, ax...  24 us
    all_to_all x1, blocking collectives, exchange(): lax.all_to_all(blocks, EVERY, split_axis=0, concat_axis=0, tiled=True, ax...  11.6 us
    ppermute x2, starting transfers between devices, swapped(): return lax.ppermute(block, 'loc', [(i, i ^ step) for i in range(LOCS)])  9.76 us
    ppermute x2, waiting for transfers between devices, swapped(): return lax.ppermute(block, 'loc', [(i, i ^ step) for i in range(LOCS)])  7.9 us
    all_to_all x2, waiting for transfers between devices, exchange(): lax.all_to_all(blocks, EVERY, split_axis=0, concat_axis=0, tiled=True, ax...  5.07 us
    pallas_call x1, Pallas kernels, on_device(): call(attend, shape(*results), vmem(2), [pltpu.VMEM(results, bf16), pltpu....  2.82 us
    all_gather x1, blocking collectives, on_device(): kv = lax.all_gather(kv, 'c', axis=0, tiled=False)  2.2 us
    pallas_call x1, Pallas kernels, on_device(): call(pack, shape(*messages), [pl.BlockSpec(memory_space=pltpu.HBM)] * 4,...  2.16 us
  transfers between devices with their start and end apart: 4, of which 4 were waited for; matrix products, arithmetic and copies ran while one was open for 0% of the time, Pallas kernels for 0%

profile of v6, /device:TPU:6, one launch (start us, length us, event | category | flops | bytes accessed | tf_op | source)
XLA Modules:
  0.0 68.2 jit_solution(17629527008657945599)
XLA Ops:
  0.0 2.2 %pack.1 = bf16[64,32,128]{2,1,0:T(8,128)(2,1)} custom-call(s32[30]{0:T(128)} %pos_hbm.1, bf16[30,1024]{1,0:T(8,128)(2,1)} %q_hbm.1, bf16[30,1024]{1,0:T(8,128)(2,1)} %k_hbm.1, bf16[30,1024]{1,0:T(8,128)(2,1)} %v_hbm.1), custom_call_target="tpu_custom_call" | custom-call | tf_op jit(solution)/shard_map/pack/pallas_call | solution.py:312
  2.2 0.0 copy-start.1
  2.2 15.2 %all-to-all-start = ((bf16[64,32,128]{2,1,0:T(8,128)(2,1)}), bf16[64,32,128]{2,1,0:T(8,128)(2,1)S(1)}, u32[]{:S(2)}, u32[]{:S(2)}) async-start(bf16[64,32,128]{2,1,0:T(8,128)(2,1)} %pack.1), calls=%async_computation | async-start | bytes 1048576 | tf_op jit(solution)/shard_map/all_to_all | solution.py:63
  17.4 0.0 copy-start.2
  17.4 0.0 copy-done.1
  17.4 0.7 copy-done.2
  18.1 0.2 pack_embed.1
  18.3 5.3 %collective-permute-start = (bf16[2,64,256]{2,1,0:T(8,128)(2,1)S(1)}, bf16[2,64,256]{2,1,0:T(8,128)(2,1)S(1)}, u32[]{:S(2)}, u32[]{:S(2)}) collective-permute-start(bf16[2,64,256]{2,1,0:T(8,128)(2,1)S(1)} %get-tuple-element.17), channel_id=1, source_target_pairs={{0,3},{1,2},{2,1},{3,0},{4,7},{5,6},{6,5},{7,4},{8,11},{9,10},{10,... | collective-permute-start | bytes 196616 | tf_op jit(solution)/shard_map/ppermute | solution.py:305
  23.6 4.2 %collective-permute-done.first_ref = bf16[2,64,256]{2,1,0:T(8,128)(2,1)S(1)} collective-permute-done((bf16[2,64,256]{2,1,0:T(8,128)(2,1)S(1)}, bf16[2,64,256]{2,1,0:T(8,128)(2,1)S(1)}, u32[]{:S(2)}, u32[]{:S(2)}) %collective-permute-start) | collective-permute-done | bytes 65568 | tf_op jit(solution)/shard_map/ppermute | solution.py:305
  27.8 4.2 %all-to-all-done.in_ref = bf16[64,32,128]{2,1,0:T(8,128)(2,1)S(1)} async-done(((bf16[64,32,128]{2,1,0:T(8,128)(2,1)}), bf16[64,32,128]{2,1,0:T(8,128)(2,1)S(1)}, u32[]{:S(2)}, u32[]{:S(2)}) %all-to-all-start) | async-done | bytes 524320 | tf_op jit(solution)/shard_map/all_to_all | solution.py:63
  32.0 0.1 split.1
  32.0 2.2 %all-gather = bf16[2176,128]{1,0:T(8,128)(2,1)S(1)} all-gather(bf16[1088,128]{1,0:T(8,128)(2,1)S(1)} %split.1), channel_id=2, replica_groups=mesh['za'=2,'zb'=2,'zc'=2,'x'=4,'yl'=2,'c'=2,'loc'=4] {'c'}, dimensions={0}, use_global_device_ids=true | all-gather | bytes 835584 | tf_op jit(solution)/shard_map/all_gather | solution.py:337
  34.2 0.0 copy-start
  34.2 2.8 %attend.1 = bf16[64,16,128]{2,1,0:T(8,128)(2,1)} custom-call(bf16[64,32,128]{2,1,0:T(8,128)(2,1)S(1)} %all-to-all-done.in_ref, bf16[2,1088,128]{2,1,0:T(8,128)(2,1)S(1)} %bitcast.3), custom_call_target="tpu_custom_call" | custom-call | flops 536870912 | bytes 524288 | tf_op jit(solution)/shard_map/attend/pallas_call | solution.py:338
  37.1 8.8 %all-to-all-start.1 = ((bf16[64,16,128]{2,1,0:T(8,128)(2,1)}), bf16[64,16,128]{2,1,0:T(8,128)(2,1)S(1)}, u32[]{:S(2)}, u32[]{:S(2)}) async-start(bf16[64,16,128]{2,1,0:T(8,128)(2,1)} %attend.1), calls=%async_computation.1 | async-start | bytes 524288 | tf_op jit(solution)/shard_map/all_to_all | solution.py:63
  45.9 4.5 %collective-permute-start.1 = (bf16[2,64,256]{2,1,0:T(8,128)(2,1)S(1)}, bf16[2,64,256]{2,1,0:T(8,128)(2,1)S(1)}, u32[]{:S(2)}, u32[]{:S(2)}) collective-permute-start(bf16[2,64,256]{2,1,0:T(8,128)(2,1)S(1)} %pad_maximum_fusion), channel_id=1, source_target_pairs={{0,1},{1,0},{2,3},{3,2},{4,5},{5,4},{6,7},{7,6},{8,9},{9,8},{10,11... | collective-permute-start | bytes 196616 | tf_op jit(solution)/shard_map/ppermute | solution.py:305
  50.4 3.7 %collective-permute-done.1.second_ref = bf16[2,64,256]{2,1,0:T(8,128)(2,1)S(1)} collective-permute-done((bf16[2,64,256]{2,1,0:T(8,128)(2,1)S(1)}, bf16[2,64,256]{2,1,0:T(8,128)(2,1)S(1)}, u32[]{:S(2)}, u32[]{:S(2)}) %collective-permute-start.1) | collective-permute-done | bytes 65568 | tf_op jit(solution)/shard_map/ppermute | solution.py:305
  54.1 0.9 %all-to-all-done.1.part_ref = bf16[64,16,128]{2,1,0:T(8,128)(2,1)S(1)} async-done(((bf16[64,16,128]{2,1,0:T(8,128)(2,1)}), bf16[64,16,128]{2,1,0:T(8,128)(2,1)S(1)}, u32[]{:S(2)}, u32[]{:S(2)}) %all-to-all-start.1) | async-done | bytes 262176 | tf_op jit(solution)/shard_map/all_to_all | solution.py:63
  55.0 0.0 copy-done
  55.0 0.8 %finish.1 = bf16[4,64,256]{2,1,0:T(8,128)(2,1)S(1)} custom-call(bf16[64,16,128]{2,1,0:T(8,128)(2,1)S(1)} %all-to-all-done.1.part_ref, bf16[512,1024]{1,0:T(8,128)(2,1)S(1)} %copy-done, bf16[64,256]{1,0:T(8,128)(2,1)S(1)} %get-tuple-element.22.own_ref, bf16[2,64,256]{2,1,0:T(8,128)(2,1)S(1)} %collective-permute-done.first_ref, ...), custom_call_target="tpu_custom_call" | custom-call | tf_op jit(solution)/shard_map/finish/pallas_call | solution.py:354
  55.7 11.6 %all_to_all.15.in_ref = bf16[4,64,256]{2,1,0:T(8,128)(2,1)S(1)} all-to-all(bf16[4,64,256]{2,1,0:T(8,128)(2,1)S(1)} %finish.1), channel_id=1, replica_groups={{2,0,1,3},{6,4,5,7},{10,8,9,11},{14,12,13,15},{18,16,17,19},{22,20,21,2..., dimensions={0} | all-to-all | bytes 262144 | tf_op jit(solution)/shard_map/all_to_all | solution.py:63
  67.3 0.9 %unpack.1 = bf16[240,256]{1,0:T(8,128)(2,1)} custom-call(bf16[4,64,256]{2,1,0:T(8,128)(2,1)S(1)} %all_to_all.15.in_ref), custom_call_target="tpu_custom_call" | custom-call | tf_op jit(solution)/shard_map/unpack/pallas_call | solution.py:361
  (2 shorter events, 0.0 us)
Async XLA Ops:
  2.2 15.2 %copy-start.1 = (bf16[240,256]{1,0:T(8,128)(2,1)S(1)}, bf16[240,256]{1,0:T(8,128)(2,1)}, u32[]{:S(2)}) copy-start(bf16[240,256]{1,0:T(8,128)(2,1)} %e_ref) | copy-start | bytes 368644
  2.2 29.8 %all-to-all-start = ((bf16[64,32,128]{2,1,0:T(8,128)(2,1)}), bf16[64,32,128]{2,1,0:T(8,128)(2,1)S(1)}, u32[]{:S(2)}, u32[]{:S(2)}) async-start(bf16[64,32,128]{2,1,0:T(8,128)(2,1)} %pack.1), calls=%async_computation | async-start | bytes 1048576 | tf_op jit(solution)/shard_map/all_to_all | solution.py:63
  17.4 0.7 %copy-start.2 = (f32[256]{0:T(256)S(1)}, f32[256]{0:T(256)}, u32[]{:S(2)}) copy-start(f32[256]{0:T(256)} %param.13) | copy-start | bytes 3076
  18.3 9.5 %collective-permute-start = (bf16[2,64,256]{2,1,0:T(8,128)(2,1)S(1)}, bf16[2,64,256]{2,1,0:T(8,128)(2,1)S(1)}, u32[]{:S(2)}, u32[]{:S(2)}) collective-permute-start(bf16[2,64,256]{2,1,0:T(8,128)(2,1)S(1)} %get-tuple-element.17), channel_id=1, source_target_pairs={{0,3},{1,2},{2,1},{3,0},{4,7},{5,6},{6,5},{7,4},{8,11},{9,10},{10,... | collective-permute-start | bytes 196616 | tf_op jit(solution)/shard_map/ppermute | solution.py:305
  34.2 20.7 %copy-start = (bf16[512,1024]{1,0:T(8,128)(2,1)S(1)}, bf16[512,1024]{1,0:T(8,128)(2,1)}, u32[]{:S(2)}) copy-start(bf16[512,1024]{1,0:T(8,128)(2,1)} %w_ref.1) | copy-start | bytes 3145732
  37.1 17.9 %all-to-all-start.1 = ((bf16[64,16,128]{2,1,0:T(8,128)(2,1)}), bf16[64,16,128]{2,1,0:T(8,128)(2,1)S(1)}, u32[]{:S(2)}, u32[]{:S(2)}) async-start(bf16[64,16,128]{2,1,0:T(8,128)(2,1)} %attend.1), calls=%async_computation.1 | async-start | bytes 524288 | tf_op jit(solution)/shard_map/all_to_all | solution.py:63
  45.9 8.2 %collective-permute-start.1 = (bf16[2,64,256]{2,1,0:T(8,128)(2,1)S(1)}, bf16[2,64,256]{2,1,0:T(8,128)(2,1)S(1)}, u32[]{:S(2)}, u32[]{:S(2)}) collective-permute-start(bf16[2,64,256]{2,1,0:T(8,128)(2,1)S(1)} %pad_maximum_fusion), channel_id=1, source_target_pairs={{0,1},{1,0},{2,3},{3,2},{4,5},{5,4},{6,7},{7,6},{8,9},{9,8},{10,11... | collective-permute-start | bytes 196616 | tf_op jit(solution)/shard_map/ppermute | solution.py:305

commit v7 on v5

--- a/solution.py
+++ b/solution.py
@@ -64,7 +64,7 @@
 
 def seq_groups(depth_order):
     return [
-        [((z * PLANE + spot) * 2 + core) * LOCS + loc for z in depth_order for spot in range(PLANE)]
+        [((z * PLANE + spot) * 2 + core) * LOCS + loc for z in depth_order for spot in range(PLANE - 1, -1, -1)]
         for core in range(2)
         for loc in range(LOCS)
     ]

time: 68.6 us -> 69.4 us (1.012)
  the two profiles are of different devices: /device:TPU:6 before, /device:TPU:1 now
where the time goes in v7:
time: 69.4 us; the launch traced here: 69 us
  starting transfers between devices  34.3 us (49%)
  waiting for transfers between devices  13.7 us (20%)
  blocking collectives  13.4 us (19%)
  Pallas kernels  6.83 us (10%)
    all_to_all x2, starting transfers between devices, exchange(): lax.all_to_all(blocks, EVERY, split_axis=0, concat_axis=0, tiled=True, ax...  25.1 us
    all_to_all x1, blocking collectives, exchange(): lax.all_to_all(blocks, EVERY, split_axis=0, concat_axis=0, tiled=True, ax...  10.2 us
    ppermute x2, starting transfers between devices, swapped(): return lax.ppermute(block, 'loc', [(i, i ^ step) for i in range(LOCS)])  9.2 us
    all_to_all x2, waiting for transfers between devices, exchange(): lax.all_to_all(blocks, EVERY, split_axis=0, concat_axis=0, tiled=True, ax...  6.9 us
    ppermute x2, waiting for transfers between devices, swapped(): return lax.ppermute(block, 'loc', [(i, i ^ step) for i in range(LOCS)])  6.78 us
    all_gather x1, blocking collectives, on_device(): kv = lax.all_gather(kv, 'c', axis=0, tiled=False)  3.2 us
    pallas_call x1, Pallas kernels, on_device(): call(attend, shape(*results), vmem(2), [pltpu.VMEM(results, bf16), pltpu....  2.82 us
    pallas_call x1, Pallas kernels, on_device(): call(pack, shape(*messages), [pl.BlockSpec(memory_space=pltpu.HBM)] * 4,...  2.08 us
  transfers between devices with their start and end apart: 4, of which 4 were waited for; matrix products, arithmetic and copies ran while one was open for 0% of the time, Pallas kernels for 0%

profile of v7, /device:TPU:1, one launch (start us, length us, event | category | flops | bytes accessed | tf_op | source)
XLA Modules:
  0.0 69.0 jit_solution(1493231859924870539)
XLA Ops:
  0.0 2.1 %pack.1 = bf16[64,32,128]{2,1,0:T(8,128)(2,1)} custom-call(s32[30]{0:T(128)} %pos_hbm.1, bf16[30,1024]{1,0:T(8,128)(2,1)} %q_hbm.1, bf16[30,1024]{1,0:T(8,128)(2,1)} %k_hbm.1, bf16[30,1024]{1,0:T(8,128)(2,1)} %v_hbm.1), custom_call_target="tpu_custom_call" | custom-call | tf_op jit(solution)/shard_map/pack/pallas_call | solution.py:305
  2.1 0.0 copy-start.1
  2.1 17.4 %all-to-all-start = ((bf16[64,32,128]{2,1,0:T(8,128)(2,1)}), bf16[64,32,128]{2,1,0:T(8,128)(2,1)S(1)}, u32[]{:S(2)}, u32[]{:S(2)}) async-start(bf16[64,32,128]{2,1,0:T(8,128)(2,1)} %pack.1), calls=%async_computation | async-start | bytes 1048576 | tf_op jit(solution)/shard_map/all_to_all | solution.py:60
  19.5 0.0 copy-start.2
  19.5 0.0 copy-done.1
  19.5 0.7 copy-done.2
  20.2 0.2 pack_embed.1
  20.4 5.0 %collective-permute-start = (bf16[2,64,256]{2,1,0:T(8,128)(2,1)S(1)}, bf16[2,64,256]{2,1,0:T(8,128)(2,1)S(1)}, u32[]{:S(2)}, u32[]{:S(2)}) collective-permute-start(bf16[2,64,256]{2,1,0:T(8,128)(2,1)S(1)} %get-tuple-element.17), channel_id=1, source_target_pairs={{0,3},{1,2},{2,1},{3,0},{4,7},{5,6},{6,5},{7,4},{8,11},{9,10},{10,... | collective-permute-start | bytes 196616 | tf_op jit(solution)/shard_map/ppermute | solution.py:298
  25.4 4.1 %collective-permute-done.first_ref = bf16[2,64,256]{2,1,0:T(8,128)(2,1)S(1)} collective-permute-done((bf16[2,64,256]{2,1,0:T(8,128)(2,1)S(1)}, bf16[2,64,256]{2,1,0:T(8,128)(2,1)S(1)}, u32[]{:S(2)}, u32[]{:S(2)}) %collective-permute-start) | collective-permute-done | bytes 65568 | tf_op jit(solution)/shard_map/ppermute | solution.py:298
  29.5 4.8 %all-to-all-done.in_ref = bf16[64,32,128]{2,1,0:T(8,128)(2,1)S(1)} async-done(((bf16[64,32,128]{2,1,0:T(8,128)(2,1)}), bf16[64,32,128]{2,1,0:T(8,128)(2,1)S(1)}, u32[]{:S(2)}, u32[]{:S(2)}) %all-to-all-start) | async-done | bytes 524320 | tf_op jit(solution)/shard_map/all_to_all | solution.py:60
  34.3 0.1 split.1
  34.4 3.2 %all-gather = bf16[2176,128]{1,0:T(8,128)(2,1)S(1)} all-gather(bf16[1088,128]{1,0:T(8,128)(2,1)S(1)} %split.1), channel_id=2, replica_groups=mesh['za'=2,'zb'=2,'zc'=2,'x'=4,'yl'=2,'c'=2,'loc'=4] {'c'}, dimensions={0}, use_global_device_ids=true | all-gather | bytes 835584 | tf_op jit(solution)/shard_map/all_gather | solution.py:330
  37.6 0.0 copy-start
  37.6 2.8 %attend.1 = bf16[64,16,128]{2,1,0:T(8,128)(2,1)} custom-call(bf16[64,32,128]{2,1,0:T(8,128)(2,1)S(1)} %all-to-all-done.in_ref, bf16[2,1088,128]{2,1,0:T(8,128)(2,1)S(1)} %bitcast.3), custom_call_target="tpu_custom_call" | custom-call | flops 536870912 | bytes 524288 | tf_op jit(solution)/shard_map/attend/pallas_call | solution.py:331
  40.4 7.8 %all-to-all-start.1 = ((bf16[64,16,128]{2,1,0:T(8,128)(2,1)}), bf16[64,16,128]{2,1,0:T(8,128)(2,1)S(1)}, u32[]{:S(2)}, u32[]{:S(2)}) async-start(bf16[64,16,128]{2,1,0:T(8,128)(2,1)} %attend.1), calls=%async_computation.1 | async-start | bytes 524288 | tf_op jit(solution)/shard_map/all_to_all | solution.py:60
  48.2 4.2 %collective-permute-start.1 = (bf16[2,64,256]{2,1,0:T(8,128)(2,1)S(1)}, bf16[2,64,256]{2,1,0:T(8,128)(2,1)S(1)}, u32[]{:S(2)}, u32[]{:S(2)}) collective-permute-start(bf16[2,64,256]{2,1,0:T(8,128)(2,1)S(1)} %pad_maximum_fusion), channel_id=1, source_target_pairs={{0,1},{1,0},{2,3},{3,2},{4,5},{5,4},{6,7},{7,6},{8,9},{9,8},{10,11... | collective-permute-start | bytes 196616 | tf_op jit(solution)/shard_map/ppermute | solution.py:298
  52.4 2.7 %collective-permute-done.1.second_ref = bf16[2,64,256]{2,1,0:T(8,128)(2,1)S(1)} collective-permute-done((bf16[2,64,256]{2,1,0:T(8,128)(2,1)S(1)}, bf16[2,64,256]{2,1,0:T(8,128)(2,1)S(1)}, u32[]{:S(2)}, u32[]{:S(2)}) %collective-permute-start.1) | collective-permute-done | bytes 65568 | tf_op jit(solution)/shard_map/ppermute | solution.py:298
  55.1 2.1 %all-to-all-done.1.part_ref = bf16[64,16,128]{2,1,0:T(8,128)(2,1)S(1)} async-done(((bf16[64,16,128]{2,1,0:T(8,128)(2,1)}), bf16[64,16,128]{2,1,0:T(8,128)(2,1)S(1)}, u32[]{:S(2)}, u32[]{:S(2)}) %all-to-all-start.1) | async-done | bytes 262176 | tf_op jit(solution)/shard_map/all_to_all | solution.py:60
  57.2 0.0 copy-done
  57.2 0.8 %finish.1 = bf16[4,64,256]{2,1,0:T(8,128)(2,1)S(1)} custom-call(bf16[64,16,128]{2,1,0:T(8,128)(2,1)S(1)} %all-to-all-done.1.part_ref, bf16[512,1024]{1,0:T(8,128)(2,1)S(1)} %copy-done, bf16[64,256]{1,0:T(8,128)(2,1)S(1)} %get-tuple-element.22.own_ref, bf16[2,64,256]{2,1,0:T(8,128)(2,1)S(1)} %collective-permute-done.first_ref, ...), custom_call_target="tpu_custom_call" | custom-call | tf_op jit(solution)/shard_map/finish/pallas_call | solution.py:347
  58.0 10.2 %all_to_all.15.in_ref = bf16[4,64,256]{2,1,0:T(8,128)(2,1)S(1)} all-to-all(bf16[4,64,256]{2,1,0:T(8,128)(2,1)S(1)} %finish.1), channel_id=1, replica_groups={{2,0,1,3},{6,4,5,7},{10,8,9,11},{14,12,13,15},{18,16,17,19},{22,20,21,2..., dimensions={0} | all-to-all | bytes 262144 | tf_op jit(solution)/shard_map/all_to_all | solution.py:60
  68.2 0.9 %unpack.1 = bf16[240,256]{1,0:T(8,128)(2,1)} custom-call(bf16[4,64,256]{2,1,0:T(8,128)(2,1)S(1)} %all_to_all.15.in_ref), custom_call_target="tpu_custom_call" | custom-call | tf_op jit(solution)/shard_map/unpack/pallas_call | solution.py:354
  (2 shorter events, 0.0 us)
Async XLA Ops:
  2.1 17.4 %copy-start.1 = (bf16[240,256]{1,0:T(8,128)(2,1)S(1)}, bf16[240,256]{1,0:T(8,128)(2,1)}, u32[]{:S(2)}) copy-start(bf16[240,256]{1,0:T(8,128)(2,1)} %e_ref) | copy-start | bytes 368644
  2.1 32.2 %all-to-all-start = ((bf16[64,32,128]{2,1,0:T(8,128)(2,1)}), bf16[64,32,128]{2,1,0:T(8,128)(2,1)S(1)}, u32[]{:S(2)}, u32[]{:S(2)}) async-start(bf16[64,32,128]{2,1,0:T(8,128)(2,1)} %pack.1), calls=%async_computation | async-start | bytes 1048576 | tf_op jit(solution)/shard_map/all_to_all | solution.py:60
  19.5 0.7 copy-start.2
  20.4 9.1 %collective-permute-start = (bf16[2,64,256]{2,1,0:T(8,128)(2,1)S(1)}, bf16[2,64,256]{2,1,0:T(8,128)(2,1)S(1)}, u32[]{:S(2)}, u32[]{:S(2)}) collective-permute-start(bf16[2,64,256]{2,1,0:T(8,128)(2,1)S(1)} %get-tuple-element.17), channel_id=1, source_target_pairs={{0,3},{1,2},{2,1},{3,0},{4,7},{5,6},{6,5},{7,4},{8,11},{9,10},{10,... | collective-permute-start | bytes 196616 | tf_op jit(solution)/shard_map/ppermute | solution.py:298
  37.6 19.6 %copy-start = (bf16[512,1024]{1,0:T(8,128)(2,1)S(1)}, bf16[512,1024]{1,0:T(8,128)(2,1)}, u32[]{:S(2)}) copy-start(bf16[512,1024]{1,0:T(8,128)(2,1)} %w_ref.1) | copy-start | bytes 3145732
  40.4 16.8 %all-to-all-start.1 = ((bf16[64,16,128]{2,1,0:T(8,128)(2,1)}), bf16[64,16,128]{2,1,0:T(8,128)(2,1)S(1)}, u32[]{:S(2)}, u32[]{:S(2)}) async-start(bf16[64,16,128]{2,1,0:T(8,128)(2,1)} %attend.1), calls=%async_computation.1 | async-start | bytes 524288 | tf_op jit(solution)/shard_map/all_to_all | solution.py:60
  48.2 6.9 %collective-permute-start.1 = (bf16[2,64,256]{2,1,0:T(8,128)(2,1)S(1)}, bf16[2,64,256]{2,1,0:T(8,128)(2,1)S(1)}, u32[]{:S(2)}, u32[]{:S(2)}) collective-permute-start(bf16[2,64,256]{2,1,0:T(8,128)(2,1)S(1)} %pad_maximum_fusion), channel_id=1, source_target_pairs={{0,1},{1,0},{2,3},{3,2},{4,5},{5,4},{6,7},{7,6},{8,9},{9,8},{10,11... | collective-permute-start | bytes 196616 | tf_op jit(solution)/shard_map/ppermute | solution.py:298
